TPU v7x, 32 devices: a whole 2x2x4 slice. The times are simulated.
32 devices in a mesh: lon: 8 (over y, x, core), lat: 4 (over z).
Axes of the slice: x: 2, y: 2, z: 4, core: 2. Of those that a mesh axis runs over, the one named last changes fastest.
Arguments:
- send_species: float32 [1024, 16, 1024], P(('lon', 'lat')), may hold values from 0.1 to 4
- send_cells: int32 [1024, 1024], P(('lon', 'lat')), may hold values from 0 to 4095
- send_counts: int32 [1024], P(('lon', 'lat')), may hold values from 0 to 1024, as said below
- grid_state: float32 [16, 8, 32, 512], P(None, None, 'lon', 'lat'), may hold values from 0.1 to 4
- diff_rate: float32 [16], replicated, may hold values from 0.04 to 0.16
- prod_rate: float32 [16, 16], replicated, may hold values from 0 to 0.3
- loss_rate: float32 [16], replicated, may hold values from 0.05 to 20
- self_rate: float32 [16], replicated, may hold values from 0.05 to 2
Outputs:
- parcels_new: float32 [1024, 16, 1024], P(('lon', 'lat'))
- grid_mixed: float32 [16, 8, 32, 512], P(None, None, 'lon', 'lat')
Inputs may be any that keep to these rules, and one draw needn't show every extreme that they name: `send_counts`: each source tile sends at most 1024 parcels to each tile. In every draw one tile receives exactly 1024 from every source, and at least a quarter of the tiles receive exactly 1024 from at least one source.
All inputs are finite; a program needn't handle non-finite values.
Results may differ from a plain program's by a relative error of at most 0.0011.
Values sent between devices are 32-bit elements; how exact they have to be, the bound alone decides.
A program may use at most 64 MiB of HBM per device.

v0:
```python
import math

import jax
import jax.numpy as jnp
from jax import lax
from jax.sharding import PartitionSpec as P

ITERS = 4
SUBSTEPS = 2


grid_weight = 0.5
parcel_pull = 0.3


def padded_2(x, sides, width):
    for axis, dim in sides:
        size, length = (lax.axis_size(axis), x.shape[dim])
        up = [(i, (i + 1) % size) for i in range(size)]
        down = [(j, i) for i, j in up]
        last = lax.slice_in_dim(x, length - width, length, axis=dim)
        initial = lax.slice_in_dim(x, 0, width, axis=dim)
        before = lax.ppermute(last, axis, up)
        after = lax.ppermute(initial, axis, down)
        x = jnp.concatenate([before, x, after], axis=dim)
    return x


def diffuse_once(padded, diff_rate, lat_first, total_lat):
    centre = padded[:, :, 1:-1, 1:-1]
    eastern = padded[:, :, 2:, 1:-1]
    western = padded[:, :, :-2, 1:-1]
    northern = padded[:, :, 1:-1, 2:]
    southern = padded[:, :, 1:-1, :-2]
    latitude = lat_first + jnp.arange(centre.shape[3], dtype=jnp.int32)
    north_open = (latitude + 1 < total_lat)[None, None, None, :]
    south_open = (latitude > 0)[None, None, None, :]
    above_cells = jnp.concatenate([centre[:, 1:], centre[:, -1:]], axis=1)
    below_cells = jnp.concatenate([centre[:, :1], centre[:, :-1]], axis=1)
    laplace = eastern + western + above_cells + below_cells - 4.0 * centre
    laplace = (
        laplace
        + jnp.where(north_open, northern - centre, 0.0)
        + jnp.where(south_open, southern - centre, 0.0)
    )
    return centre + diff_rate[:, None, None, None] * laplace


def hot_tables(cell_block, high_size, low_size):
    high_index = cell_block // low_size
    low_index = cell_block % low_size
    high_hot = (jnp.arange(high_size, dtype=jnp.int32)[:, None] == high_index[None, :]).astype(
        jnp.bfloat16
    )
    low_hot = (low_index[:, None] == jnp.arange(low_size, dtype=jnp.int32)[None, :]).astype(
        jnp.bfloat16
    )
    return (high_hot, low_hot)


def local(
    send_species, send_cells, send_counts, grid_state, diff_rate, prod_rate, loss_rate, self_rate
):
    lat_count = lax.axis_size("lat")
    species_count = send_species.shape[1]
    capacity = send_species.shape[2]
    slot_index = jnp.arange(capacity, dtype=jnp.int32)[None, :]
    marked = jnp.where(slot_index < send_counts[:, None], send_cells, -1)
    arrived, cell_ids = (
        lax.all_to_all(send_species, ("lon", "lat"), split_axis=0, concat_axis=0, tiled=True),
        lax.all_to_all(marked, ("lon", "lat"), split_axis=0, concat_axis=0, tiled=True),
    )
    levels = grid_state.shape[1]
    lon_cols = grid_state.shape[2]
    lat_cols = grid_state.shape[3]
    total_lat = lat_count * lat_cols
    lat_base = lax.axis_index("lat") * lat_cols
    diffused = grid_state
    for substep in range(SUBSTEPS):
        padded = padded_2(diffused, (("lon", 2), ("lat", 3)), 1)
        diffused = diffuse_once(padded, diff_rate, lat_base, total_lat)
    high_size = levels * lon_cols
    total = arrived.shape[0] * capacity
    block_size = math.gcd(total, 2048)
    turn_count = total // block_size
    flat_species = (
        arrived.transpose(1, 0, 2).reshape(species_count, turn_count, block_size).transpose(1, 0, 2)
    )
    flat_cells = cell_ids.reshape(turn_count, block_size)

    def deposit_block(running, inputs):
        deposit_sum, number = running
        block_species, cell_block = inputs
        high_hot, low_hot = hot_tables(cell_block, high_size, lat_cols)
        spread = block_species.astype(jnp.bfloat16)[:, None, :] * high_hot[None, :, :]
        deposit_sum = deposit_sum + jnp.einsum(
            "shb,bl->shl", spread, low_hot, preferred_element_type=jnp.float32
        )
        number = number + jnp.dot(high_hot, low_hot, preferred_element_type=jnp.float32)
        return ((deposit_sum, number), None)

    start_sum = (
        jnp.zeros((species_count, high_size, lat_cols), jnp.float32),
        jnp.zeros((high_size, lat_cols), jnp.float32),
    )
    (deposit_sum, number), unused = lax.scan(deposit_block, start_sum, (flat_species, flat_cells))
    grid_mixed = (diffused + grid_weight * deposit_sum.reshape(grid_state.shape)) / (
        1.0 + grid_weight * number.reshape(1, levels, lon_cols, lat_cols)
    )
    coarse = grid_mixed.astype(jnp.bfloat16).reshape(species_count, high_size, lat_cols)

    def react_block(running, inputs):
        block_species, cell_block = inputs
        high_hot, low_hot = hot_tables(cell_block, high_size, lat_cols)
        picked = jnp.einsum("shl,bl->shb", coarse, low_hot, preferred_element_type=jnp.float32)
        at_parcel = jnp.sum(picked * high_hot[None, :, :].astype(jnp.float32), axis=1)
        blended = block_species + parcel_pull * (at_parcel - block_species)
        concentration = blended
        for sweep in range(ITERS):
            produced = blended + jnp.dot(prod_rate, concentration, precision=lax.Precision.HIGHEST)
            concentration = produced / (
                1.0 + loss_rate[:, None] + self_rate[:, None] * concentration
            )
        reacted = jnp.where((cell_block >= 0)[None, :], concentration, 0.0)
        return (running, reacted)

    unused, reacted = lax.scan(react_block, jnp.zeros((), jnp.float32), (flat_species, flat_cells))
    parcels_new = (
        reacted.transpose(1, 0, 2)
        .reshape(species_count, arrived.shape[0], capacity)
        .transpose(1, 0, 2)
    )
    return (parcels_new, grid_mixed)


def solution(mesh):
    placed = (
        P(("lon", "lat"), None, None),
        P(("lon", "lat"), None),
        P(("lon", "lat")),
        P(None, None, "lon", "lat"),
        P(),
        P(),
        P(),
        P(),
    )
    return jax.shard_map(
        local,
        mesh=mesh,
        in_specs=placed,
        out_specs=(P(("lon", "lat"), None, None), P(None, None, "lon", "lat")),
        check_vma=False,
    )
```

profile of v0, /device:TPU:0, one launch (start us, length us, event | category | flops | bytes accessed | tf_op | source)
XLA Modules:
  0.0 234.7 jit_solution(13173454856835019877)
XLA Ops:
  0.6 1.0 fusion.60
  1.7 15.5 %all_to_all.14 = s32[32,1,1024]{2,1,0:T(1,128)S(1)} all-to-all(s32[32,1,1024]{2,1,0:T(1,128)S(1)} %all_to_all.9), channel_id=1, replica_groups=mesh['lon'=8,'lat'=4] {'lon','lat'}, dimensions={0} | all-to-all | bytes 262144 | tf_op jit(solution)/shard_map/all_to_all | solution.py:71
  17.2 2.9 %all-to-all-start.1 = ((f32[32,16,1024]{2,1,0:T(8,128)}), f32[32,16,1024]{2,1,0:T(8,128)S(1)}, u32[]{:S(2)}, u32[]{:S(2)}) async-start(f32[32,16,1024]{2,1,0:T(8,128)} %param.12), calls=%async_computation.1 | async-start | bytes 4194304 | tf_op jit(solution)/shard_map/all_to_all | solution.py:70
  20.2 2.4 %collective-permute-start = (f32[16,8,1,128]{3,2,1,0:T(1,128)S(1)}, f32[16,8,1,128]{3,2,1,0:T(1,128)S(1)}, u32[]{:S(2)}, u32[]{:S(2)}) collective-permute-start(f32[16,8,1,128]{3,2,1,0:T(1,128)S(1)} %get-tuple-element.275), channel_id=1, source_target_pairs={{4,0},{8,4},{12,8},{16,12},{20,16},{24,20},{28,24},{0,28},{5,1},{9... | collective-permute-start | bytes 196616 | tf_op jit(solution)/shard_map/ppermute | solution.py:24
  22.7 10.7 %collective-permute-done = f32[16,8,1,128]{3,2,1,0:T(1,128)S(1)} collective-permute-done((f32[16,8,1,128]{3,2,1,0:T(1,128)S(1)}, f32[16,8,1,128]{3,2,1,0:T(1,128)S(1)}, u32[]{:S(2)}, u32[]{:S(2)}) %collective-permute-start) | collective-permute-done | bytes 65568 | tf_op jit(solution)/shard_map/ppermute | solution.py:24
  33.4 4.7 %collective-permute-done.1 = f32[16,8,1,128]{3,2,1,0:T(1,128)S(1)} collective-permute-done((f32[16,8,1,128]{3,2,1,0:T(1,128)S(1)}, f32[16,8,1,128]{3,2,1,0:T(1,128)S(1)}, u32[]{:S(2)}, u32[]{:S(2)}) %collective-permute-start.1) | collective-permute-done | bytes 65568 | tf_op jit(solution)/shard_map/ppermute | solution.py:23
  38.3 1.1 fusion.66
  39.4 4.1 %collective-permute-start.2 = (f32[16,8,6,1]{3,2,1,0:T(8,128)}, f32[16,8,6,1]{3,2,1,0:T(8,128)}, u32[]{:S(2)}, u32[]{:S(2)}) collective-permute-start(f32[16,8,6,1]{3,2,1,0:T(8,128)} %get-tuple-element.262), channel_id=1, source_target_pairs={{1,0},{2,1},{3,2},{0,3},{5,4},{6,5},{7,6},{4,7},{9,8},{10,9},{11,1... | collective-permute-start | bytes 9224 | tf_op jit(solution)/shard_map/ppermute | solution.py:24
  43.6 25.4 %collective-permute-done.2 = f32[16,8,6,1]{3,2,1,0:T(8,128)} collective-permute-done((f32[16,8,6,1]{3,2,1,0:T(8,128)}, f32[16,8,6,1]{3,2,1,0:T(8,128)}, u32[]{:S(2)}, u32[]{:S(2)}) %collective-permute-start.2) | collective-permute-done | bytes 3104 | tf_op jit(solution)/shard_map/ppermute | solution.py:24
  69.1 12.9 %collective-permute-done.3 = f32[16,8,6,1]{3,2,1,0:T(8,128)} collective-permute-done((f32[16,8,6,1]{3,2,1,0:T(8,128)}, f32[16,8,6,1]{3,2,1,0:T(8,128)}, u32[]{:S(2)}, u32[]{:S(2)}) %collective-permute-start.3) | collective-permute-done | bytes 3104 | tf_op jit(solution)/shard_map/ppermute | solution.py:23
  81.9 2.2 fusion.52
  84.3 1.1 collective-permute-start.4
  87.5 2.5 %collective-permute-done.5 = f32[16,8,1,128]{3,2,1,0:T(1,128)S(1)} collective-permute-done((f32[16,8,1,128]{3,2,1,0:T(1,128)S(1)}, f32[16,8,1,128]{3,2,1,0:T(1,128)S(1)}, u32[]{:S(2)}, u32[]{:S(2)}) %collective-permute-start.5) | collective-permute-done | bytes 65568 | tf_op jit(solution)/shard_map/ppermute | solution.py:23
  90.1 1.1 fusion.65
  91.6 10.6 %collective-permute-start.7 = (f32[16,8,6,1]{3,2,1,0:T(8,128)}, f32[16,8,6,1]{3,2,1,0:T(8,128)}, u32[]{:S(2)}, u32[]{:S(2)}) collective-permute-start(f32[16,8,6,1]{3,2,1,0:T(8,128)} %get-tuple-element.261), channel_id=1, source_target_pairs={{0,1},{1,2},{2,3},{3,0},{4,5},{5,6},{6,7},{7,4},{8,9},{9,10},{10,1... | collective-permute-start | bytes 9224 | tf_op jit(solution)/shard_map/ppermute | solution.py:23
  102.6 2.6 %copy.15 = f32[16,32,1024]{2,1,0:T(8,128)} copy(f32[16,32,1024]{2,0,1:T(8,128)S(1)} %bitcast.119) | data formatting | bytes 4194304 | tf_op jit(solution)/shard_map/transpose | solution.py:87
  105.1 1.9 reshape.145
  107.1 2.6 %fusion.64 = (bf16[16,16,2048]{2,1,0:T(8,128)(2,1)S(1)}, f32[16,16,2048]{2,1,0:T(8,128)}) fusion(f32[16,16,2048]{2,0,1:T(8,128)S(1)} %bitcast.120), kind=kLoop, calls=%fused_computation.113 | loop fusion | flops 524288 | bytes 5242880
  109.7 49.1 %while.28 = (s32[]{:T(128)}, f32[16,32,128]{2,1,0:T(8,128)}, f32[32,128]{1,0:T(8,128)S(1)}, bf16[16,16,2048]{2,1,0:T(8,128)(2,1)S(1)}, s32[16,2048]{1,0:T(8,128)S(1)}, /*index=5*/s32[]{:T(128)}, s32[]{:T(128)}) while((s32[]{:T(128)}, f32[16,32,128]{2,1,0:T(8,128)}, f32[32,128]{1,0:T(8,128)S(1)}, ...), condition=%wide.region_1.2_spmd.clone, body=%wide.region_0.1_spmd.clone.sunk | while | flops 287174656 | bytes 1089632 | solution.py:106
  109.9 1.6 fusion.123
  112.1 2.5 %fusion.123 = f32[16,32,128]{2,1,0:T(8,128)} fusion(bf16[32,2048]{1,0:T(8,128)(2,1)S(1)} %fusion.121, bf16[16,2048]{1,0:T(8,128)(2,1)S(1)} %fusion.122, s32[2048]{0:T(1024)S(1)} %add_select_fusion.5, f32[16,32,128]{2,1,0:T(8,128)} %get-tuple-element.374, pred[]{:T(512)S(6)} %compare.21), kind=kOutput, calls=%fused_computation.2.clone.1 | convolution fusion | flops 269877248 | bytes 729089 | tf_op jit(solution)/shard_map/while/body/eval_jaxpr/shb,bl->shl/dot_general | solution.py:96
  115.2 2.5 %fusion.123 = f32[16,32,128]{2,1,0:T(8,128)} fusion(bf16[32,2048]{1,0:T(8,128)(2,1)S(1)} %fusion.121, bf16[16,2048]{1,0:T(8,128)(2,1)S(1)} %fusion.122, s32[2048]{0:T(1024)S(1)} %add_select_fusion.5, f32[16,32,128]{2,1,0:T(8,128)} %get-tuple-element.374, pred[]{:T(512)S(6)} %compare.21), kind=kOutput, calls=%fused_computation.2.clone.1 | convolution fusion | flops 269877248 | bytes 729089 | tf_op jit(solution)/shard_map/while/body/eval_jaxpr/shb,bl->shl/dot_general | solution.py:96
  118.3 2.5 %fusion.123 = f32[16,32,128]{2,1,0:T(8,128)} fusion(bf16[32,2048]{1,0:T(8,128)(2,1)S(1)} %fusion.121, bf16[16,2048]{1,0:T(8,128)(2,1)S(1)} %fusion.122, s32[2048]{0:T(1024)S(1)} %add_select_fusion.5, f32[16,32,128]{2,1,0:T(8,128)} %get-tuple-element.374, pred[]{:T(512)S(6)} %compare.21), kind=kOutput, calls=%fused_computation.2.clone.1 | convolution fusion | flops 269877248 | bytes 729089 | tf_op jit(solution)/shard_map/while/body/eval_jaxpr/shb,bl->shl/dot_general | solution.py:96
  121.5 2.5 %fusion.123 = f32[16,32,128]{2,1,0:T(8,128)} fusion(bf16[32,2048]{1,0:T(8,128)(2,1)S(1)} %fusion.121, bf16[16,2048]{1,0:T(8,128)(2,1)S(1)} %fusion.122, s32[2048]{0:T(1024)S(1)} %add_select_fusion.5, f32[16,32,128]{2,1,0:T(8,128)} %get-tuple-element.374, pred[]{:T(512)S(6)} %compare.21), kind=kOutput, calls=%fused_computation.2.clone.1 | convolution fusion | flops 269877248 | bytes 729089 | tf_op jit(solution)/shard_map/while/body/eval_jaxpr/shb,bl->shl/dot_general | solution.py:96
  124.6 2.5 %fusion.123 = f32[16,32,128]{2,1,0:T(8,128)} fusion(bf16[32,2048]{1,0:T(8,128)(2,1)S(1)} %fusion.121, bf16[16,2048]{1,0:T(8,128)(2,1)S(1)} %fusion.122, s32[2048]{0:T(1024)S(1)} %add_select_fusion.5, f32[16,32,128]{2,1,0:T(8,128)} %get-tuple-element.374, pred[]{:T(512)S(6)} %compare.21), kind=kOutput, calls=%fused_computation.2.clone.1 | convolution fusion | flops 269877248 | bytes 729089 | tf_op jit(solution)/shard_map/while/body/eval_jaxpr/shb,bl->shl/dot_general | solution.py:96
  127.7 2.5 %fusion.123 = f32[16,32,128]{2,1,0:T(8,128)} fusion(bf16[32,2048]{1,0:T(8,128)(2,1)S(1)} %fusion.121, bf16[16,2048]{1,0:T(8,128)(2,1)S(1)} %fusion.122, s32[2048]{0:T(1024)S(1)} %add_select_fusion.5, f32[16,32,128]{2,1,0:T(8,128)} %get-tuple-element.374, pred[]{:T(512)S(6)} %compare.21), kind=kOutput, calls=%fused_computation.2.clone.1 | convolution fusion | flops 269877248 | bytes 729089 | tf_op jit(solution)/shard_map/while/body/eval_jaxpr/shb,bl->shl/dot_general | solution.py:96
  130.8 2.5 %fusion.123 = f32[16,32,128]{2,1,0:T(8,128)} fusion(bf16[32,2048]{1,0:T(8,128)(2,1)S(1)} %fusion.121, bf16[16,2048]{1,0:T(8,128)(2,1)S(1)} %fusion.122, s32[2048]{0:T(1024)S(1)} %add_select_fusion.5, f32[16,32,128]{2,1,0:T(8,128)} %get-tuple-element.374, pred[]{:T(512)S(6)} %compare.21), kind=kOutput, calls=%fused_computation.2.clone.1 | convolution fusion | flops 269877248 | bytes 729089 | tf_op jit(solution)/shard_map/while/body/eval_jaxpr/shb,bl->shl/dot_general | solution.py:96
  134.0 2.5 %fusion.123 = f32[16,32,128]{2,1,0:T(8,128)} fusion(bf16[32,2048]{1,0:T(8,128)(2,1)S(1)} %fusion.121, bf16[16,2048]{1,0:T(8,128)(2,1)S(1)} %fusion.122, s32[2048]{0:T(1024)S(1)} %add_select_fusion.5, f32[16,32,128]{2,1,0:T(8,128)} %get-tuple-element.374, pred[]{:T(512)S(6)} %compare.21), kind=kOutput, calls=%fused_computation.2.clone.1 | convolution fusion | flops 269877248 | bytes 729089 | tf_op jit(solution)/shard_map/while/body/eval_jaxpr/shb,bl->shl/dot_general | solution.py:96
  137.1 2.5 %fusion.123 = f32[16,32,128]{2,1,0:T(8,128)} fusion(bf16[32,2048]{1,0:T(8,128)(2,1)S(1)} %fusion.121, bf16[16,2048]{1,0:T(8,128)(2,1)S(1)} %fusion.122, s32[2048]{0:T(1024)S(1)} %add_select_fusion.5, f32[16,32,128]{2,1,0:T(8,128)} %get-tuple-element.374, pred[]{:T(512)S(6)} %compare.21), kind=kOutput, calls=%fused_computation.2.clone.1 | convolution fusion | flops 269877248 | bytes 729089 | tf_op jit(solution)/shard_map/while/body/eval_jaxpr/shb,bl->shl/dot_general | solution.py:96
  140.2 2.5 %fusion.123 = f32[16,32,128]{2,1,0:T(8,128)} fusion(bf16[32,2048]{1,0:T(8,128)(2,1)S(1)} %fusion.121, bf16[16,2048]{1,0:T(8,128)(2,1)S(1)} %fusion.122, s32[2048]{0:T(1024)S(1)} %add_select_fusion.5, f32[16,32,128]{2,1,0:T(8,128)} %get-tuple-element.374, pred[]{:T(512)S(6)} %compare.21), kind=kOutput, calls=%fused_computation.2.clone.1 | convolution fusion | flops 269877248 | bytes 729089 | tf_op jit(solution)/shard_map/while/body/eval_jaxpr/shb,bl->shl/dot_general | solution.py:96
  143.3 2.5 %fusion.123 = f32[16,32,128]{2,1,0:T(8,128)} fusion(bf16[32,2048]{1,0:T(8,128)(2,1)S(1)} %fusion.121, bf16[16,2048]{1,0:T(8,128)(2,1)S(1)} %fusion.122, s32[2048]{0:T(1024)S(1)} %add_select_fusion.5, f32[16,32,128]{2,1,0:T(8,128)} %get-tuple-element.374, pred[]{:T(512)S(6)} %compare.21), kind=kOutput, calls=%fused_computation.2.clone.1 | convolution fusion | flops 269877248 | bytes 729089 | tf_op jit(solution)/shard_map/while/body/eval_jaxpr/shb,bl->shl/dot_general | solution.py:96
  146.5 2.5 %fusion.123 = f32[16,32,128]{2,1,0:T(8,128)} fusion(bf16[32,2048]{1,0:T(8,128)(2,1)S(1)} %fusion.121, bf16[16,2048]{1,0:T(8,128)(2,1)S(1)} %fusion.122, s32[2048]{0:T(1024)S(1)} %add_select_fusion.5, f32[16,32,128]{2,1,0:T(8,128)} %get-tuple-element.374, pred[]{:T(512)S(6)} %compare.21), kind=kOutput, calls=%fused_computation.2.clone.1 | convolution fusion | flops 269877248 | bytes 729089 | tf_op jit(solution)/shard_map/while/body/eval_jaxpr/shb,bl->shl/dot_general | solution.py:96
  149.6 2.5 %fusion.123 = f32[16,32,128]{2,1,0:T(8,128)} fusion(bf16[32,2048]{1,0:T(8,128)(2,1)S(1)} %fusion.121, bf16[16,2048]{1,0:T(8,128)(2,1)S(1)} %fusion.122, s32[2048]{0:T(1024)S(1)} %add_select_fusion.5, f32[16,32,128]{2,1,0:T(8,128)} %get-tuple-element.374, pred[]{:T(512)S(6)} %compare.21), kind=kOutput, calls=%fused_computation.2.clone.1 | convolution fusion | flops 269877248 | bytes 729089 | tf_op jit(solution)/shard_map/while/body/eval_jaxpr/shb,bl->shl/dot_general | solution.py:96
  152.7 2.5 %fusion.123 = f32[16,32,128]{2,1,0:T(8,128)} fusion(bf16[32,2048]{1,0:T(8,128)(2,1)S(1)} %fusion.121, bf16[16,2048]{1,0:T(8,128)(2,1)S(1)} %fusion.122, s32[2048]{0:T(1024)S(1)} %add_select_fusion.5, f32[16,32,128]{2,1,0:T(8,128)} %get-tuple-element.374, pred[]{:T(512)S(6)} %compare.21), kind=kOutput, calls=%fused_computation.2.clone.1 | convolution fusion | flops 269877248 | bytes 729089 | tf_op jit(solution)/shard_map/while/body/eval_jaxpr/shb,bl->shl/dot_general | solution.py:96
  155.9 2.5 %fusion.123 = f32[16,32,128]{2,1,0:T(8,128)} fusion(bf16[32,2048]{1,0:T(8,128)(2,1)S(1)} %fusion.121, bf16[16,2048]{1,0:T(8,128)(2,1)S(1)} %fusion.122, s32[2048]{0:T(1024)S(1)} %add_select_fusion.5, f32[16,32,128]{2,1,0:T(8,128)} %get-tuple-element.374, pred[]{:T(512)S(6)} %compare.21), kind=kOutput, calls=%fused_computation.2.clone.1 | convolution fusion | flops 269877248 | bytes 729089 | tf_op jit(solution)/shard_map/while/body/eval_jaxpr/shb,bl->shl/dot_general | solution.py:96
  158.9 1.0 broadcast_multiply_fusion
  160.0 3.0 %fusion.62 = (bf16[16,8,4,128]{3,2,1,0:T(4,128)(2,1)S(1)}, f32[16,8,4,128]{3,2,1,0:T(4,128)}) fusion(f32[8,4,128]{2,1,0:T(4,128)S(1)} %bitcast.130, f32[16,8,4,128]{3,2,1,0:T(4,128)S(1)} %bitcast.124, f32[16,8,4,128]{3,2,1,0:T(4,128)S(1)} %fusion.52, f32[16,8,1,128]{3,2,1,0:T(1,128)S(1)} %copy-done.4, f32[16,8,1,128]{3,2,1,0:T(1,128)S(1)} %copy-done.6, ...), kind=kLoop, calls=%fused_computation.112 | loop fusion | flops 1703936 | bytes 1595712 | tf_op jit(solution)/shard_map/convert_element_type | solution.py:110
  163.0 63.2 %while.27 = (s32[]{:T(128)}, f32[16,16,2048]{2,1,0:T(8,128)}, s32[16,2048]{1,0:T(8,128)S(1)}, f32[16,16,2048]{2,1,0:T(8,128)}, bf16[16,32,128]{2,1,0:T(8,128)(2,...) while((s32[]{:T(128)}, f32[16,16,2048]{2,1,0:T(8,128)}, ...), condition=%wide.region_4.5_spmd, body=%wide.region_2.4_spmd.sunk | while | flops 296835072 | bytes 2835557 | solution.py:127
  163.2 1.2 fusion.114
  164.3 0.9 bitcast_add_fusion.2
  167.1 1.2 fusion.114
  168.3 0.9 bitcast_add_fusion.2
  171.1 1.2 fusion.114
  172.2 0.9 bitcast_add_fusion.2
  175.0 1.2 fusion.114
  176.2 0.9 bitcast_add_fusion.2
  179.0 1.2 fusion.114
  180.1 0.9 bitcast_add_fusion.2
  182.9 1.2 fusion.114
  186.9 1.2 fusion.114
  190.8 1.2 fusion.114
  194.8 1.2 fusion.114
  198.7 1.2 fusion.114
  202.7 1.2 fusion.114
  203.8 0.9 bitcast_add_fusion.2
  206.6 1.2 fusion.114
  207.8 0.9 bitcast_add_fusion.2
  210.6 1.2 fusion.114
  214.5 1.2 fusion.114
  218.5 1.2 fusion.114
  222.4 1.2 fusion.114
  226.2 2.8 %copy.18 = f32[16,16,2048]{2,1,0:T(8,128)S(1)} copy(f32[16,16,2048]{2,0,1:T(8,128)} %bitcast.122) | data formatting | bytes 4194304 | tf_op jit(solution)/shard_map/transpose | solution.py:129
  229.0 1.5 reshape.147
  230.6 4.1 %copy.19 = f32[32,16,1024]{2,1,0:T(8,128)} copy(f32[32,16,1024]{2,0,1:T(8,128)} %bitcast.121) | data formatting | bytes 4194304
  (293 shorter events, 49.8 us)
Async XLA Ops:
  17.2 2.9 %copy-start = (f32[16,8,4,128]{3,2,1,0:T(4,128)S(1)}, f32[16,8,4,128]{3,2,1,0:T(4,128)}, u32[]{:S(2)}) copy-start(f32[16,8,4,128]{3,2,1,0:T(4,128)} %param.15) | copy-start | bytes 786436
  17.2 85.3 %all-to-all-start.1 = ((f32[32,16,1024]{2,1,0:T(8,128)}), f32[32,16,1024]{2,1,0:T(8,128)S(1)}, u32[]{:S(2)}, u32[]{:S(2)}) async-start(f32[32,16,1024]{2,1,0:T(8,128)} %param.12), calls=%async_computation.1 | async-start | bytes 4194304 | tf_op jit(solution)/shard_map/all_to_all | solution.py:70
  20.2 61.7 %copy-start.9 = (f32[16]{0:T(128)S(1)}, f32[16]{0:T(128)}, u32[]{:S(2)}) copy-start(f32[16]{0:T(128)} %param.16) | copy-start | bytes 196
  20.2 13.2 %collective-permute-start = (f32[16,8,1,128]{3,2,1,0:T(1,128)S(1)}, f32[16,8,1,128]{3,2,1,0:T(1,128)S(1)}, u32[]{:S(2)}, u32[]{:S(2)}) collective-permute-start(f32[16,8,1,128]{3,2,1,0:T(1,128)S(1)} %get-tuple-element.275), channel_id=1, source_target_pairs={{4,0},{8,4},{12,8},{16,12},{20,16},{24,20},{28,24},{0,28},{5,1},{9... | collective-permute-start | bytes 196616 | tf_op jit(solution)/shard_map/ppermute | solution.py:24
  22.6 15.5 %collective-permute-start.1 = (f32[16,8,1,128]{3,2,1,0:T(1,128)S(1)}, f32[16,8,1,128]{3,2,1,0:T(1,128)S(1)}, u32[]{:S(2)}, u32[]{:S(2)}) collective-permute-start(f32[16,8,1,128]{3,2,1,0:T(1,128)S(1)} %get-tuple-element.274), channel_id=1, source_target_pairs={{0,4},{4,8},{8,12},{12,16},{16,20},{20,24},{24,28},{28,0},{1,5},{5... | collective-permute-start | bytes 196616 | tf_op jit(solution)/shard_map/ppermute | solution.py:23
  39.4 29.6 %collective-permute-start.2 = (f32[16,8,6,1]{3,2,1,0:T(8,128)}, f32[16,8,6,1]{3,2,1,0:T(8,128)}, u32[]{:S(2)}, u32[]{:S(2)}) collective-permute-start(f32[16,8,6,1]{3,2,1,0:T(8,128)} %get-tuple-element.262), channel_id=1, source_target_pairs={{1,0},{2,1},{3,2},{0,3},{5,4},{6,5},{7,6},{4,7},{9,8},{10,9},{11,1... | collective-permute-start | bytes 9224 | tf_op jit(solution)/shard_map/ppermute | solution.py:24
  43.6 38.3 %collective-permute-start.3 = (f32[16,8,6,1]{3,2,1,0:T(8,128)}, f32[16,8,6,1]{3,2,1,0:T(8,128)}, u32[]{:S(2)}, u32[]{:S(2)}) collective-permute-start(f32[16,8,6,1]{3,2,1,0:T(8,128)} %get-tuple-element.263), channel_id=1, source_target_pairs={{0,1},{1,2},{2,3},{3,0},{4,5},{5,6},{6,7},{7,4},{8,9},{9,10},{10,1... | collective-permute-start | bytes 9224 | tf_op jit(solution)/shard_map/ppermute | solution.py:23
  43.6 46.5 %copy-start.11 = (pred[128]{0:T(512)(128)(4,1)}, pred[128]{0:T(512)(128)(4,1)S(1)}, u32[]{:S(2)}) copy-start(pred[128]{0:T(512)(128)(4,1)S(1)} %get-tuple-element.276) | copy-start | bytes 388
  43.6 46.5 %copy-start.13 = (pred[128]{0:T(512)(128)(4,1)}, pred[128]{0:T(512)(128)(4,1)S(1)}, u32[]{:S(2)}) copy-start(pred[128]{0:T(512)(128)(4,1)S(1)} %get-tuple-element.277) | copy-start | bytes 388
  84.3 3.2 %collective-permute-start.4 = (f32[16,8,1,128]{3,2,1,0:T(1,128)S(1)}, f32[16,8,1,128]{3,2,1,0:T(1,128)S(1)}, u32[]{:S(2)}, u32[]{:S(2)}) collective-permute-start(f32[16,8,1,128]{3,2,1,0:T(1,128)S(1)} %get-tuple-element.269), channel_id=1, source_target_pairs={{4,0},{8,4},{12,8},{16,12},{20,16},{24,20},{28,24},{0,28},{5,1},{9... | collective-permute-start | bytes 196616 | tf_op jit(solution)/shard_map/ppermute | solution.py:24
  85.3 4.6 %collective-permute-start.5 = (f32[16,8,1,128]{3,2,1,0:T(1,128)S(1)}, f32[16,8,1,128]{3,2,1,0:T(1,128)S(1)}, u32[]{:S(2)}, u32[]{:S(2)}) collective-permute-start(f32[16,8,1,128]{3,2,1,0:T(1,128)S(1)} %get-tuple-element.268), channel_id=1, source_target_pairs={{0,4},{4,8},{8,12},{12,16},{16,20},{20,24},{24,28},{28,0},{1,5},{5... | collective-permute-start | bytes 196616 | tf_op jit(solution)/shard_map/ppermute | solution.py:23
  87.5 4.1 %copy-start.3 = (f32[16,8,1,128]{3,2,1,0:T(1,128)}, f32[16,8,1,128]{3,2,1,0:T(1,128)S(1)}, u32[]{:S(2)}) copy-start(f32[16,8,1,128]{3,2,1,0:T(1,128)S(1)} %collective-permute-done.4) | copy-start | bytes 196612
  89.9 1.6 copy-start.5
  91.3 68.6 %collective-permute-start.6 = (f32[16,8,6,1]{3,2,1,0:T(8,128)}, f32[16,8,6,1]{3,2,1,0:T(8,128)}, u32[]{:S(2)}, u32[]{:S(2)}) collective-permute-start(f32[16,8,6,1]{3,2,1,0:T(8,128)} %get-tuple-element.260), channel_id=1, source_target_pairs={{1,0},{2,1},{3,2},{0,3},{5,4},{6,5},{7,6},{4,7},{9,8},{10,9},{11,1... | collective-permute-start | bytes 9224 | tf_op jit(solution)/shard_map/ppermute | solution.py:24
  91.6 68.3 %collective-permute-start.7 = (f32[16,8,6,1]{3,2,1,0:T(8,128)}, f32[16,8,6,1]{3,2,1,0:T(8,128)}, u32[]{:S(2)}, u32[]{:S(2)}) collective-permute-start(f32[16,8,6,1]{3,2,1,0:T(8,128)} %get-tuple-element.261), channel_id=1, source_target_pairs={{0,1},{1,2},{2,3},{3,0},{4,5},{5,6},{6,7},{7,4},{8,9},{9,10},{10,1... | collective-permute-start | bytes 9224 | tf_op jit(solution)/shard_map/ppermute | solution.py:23
  109.7 50.2 %copy-start.1 = (f32[16,7,4,128]{3,2,1,0:T(4,128)S(1)}, f32[16,7,4,128]{3,2,1,0:T(4,128)}, u32[]{:S(2)}) copy-start(f32[16,7,4,128]{3,2,1,0:T(4,128)} %get-tuple-element.264) | copy-start | bytes 688132
  109.7 50.2 %copy-start.2 = (f32[16,7,4,128]{3,2,1,0:T(4,128)S(1)}, f32[16,7,4,128]{3,2,1,0:T(4,128)}, u32[]{:S(2)}) copy-start(f32[16,7,4,128]{3,2,1,0:T(4,128)} %get-tuple-element.265) | copy-start | bytes 688132
  109.7 50.2 %copy-start.4 = (f32[16,8,1,128]{3,2,1,0:T(1,128)S(1)}, f32[16,8,1,128]{3,2,1,0:T(1,128)}, u32[]{:S(2)}) copy-start(f32[16,8,1,128]{3,2,1,0:T(1,128)} %copy-done.3) | copy-start | bytes 196612
  109.7 50.2 %copy-start.6 = (f32[16,8,1,128]{3,2,1,0:T(1,128)S(1)}, f32[16,8,1,128]{3,2,1,0:T(1,128)}, u32[]{:S(2)}) copy-start(f32[16,8,1,128]{3,2,1,0:T(1,128)} %copy-done.5) | copy-start | bytes 196612
  109.7 50.2 %copy-start.7 = (f32[16,1,4,128]{3,2,1,0:T(4,128)S(1)}, f32[16,1,4,128]{3,2,1,0:T(4,128)}, u32[]{:S(2)}) copy-start(f32[16,1,4,128]{3,2,1,0:T(4,128)} %get-tuple-element.266) | copy-start | bytes 98308
  109.7 50.2 %copy-start.8 = (f32[16,1,4,128]{3,2,1,0:T(4,128)S(1)}, f32[16,1,4,128]{3,2,1,0:T(4,128)}, u32[]{:S(2)}) copy-start(f32[16,1,4,128]{3,2,1,0:T(4,128)} %get-tuple-element.267) | copy-start | bytes 98308
  109.7 50.2 %copy-start.10 = (f32[16]{0:T(128)S(1)}, f32[16]{0:T(128)}, u32[]{:S(2)}) copy-start(f32[16]{0:T(128)} %param.16) | copy-start | bytes 196
  109.7 50.2 %copy-start.12 = (pred[128]{0:T(512)(128)(4,1)S(1)}, pred[128]{0:T(512)(128)(4,1)}, u32[]{:S(2)}) copy-start(pred[128]{0:T(512)(128)(4,1)} %copy-done.11) | copy-start | bytes 388
  109.7 50.2 %copy-start.14 = (pred[128]{0:T(512)(128)(4,1)S(1)}, pred[128]{0:T(512)(128)(4,1)}, u32[]{:S(2)}) copy-start(pred[128]{0:T(512)(128)(4,1)} %copy-done.13) | copy-start | bytes 388
  158.8 4.2 %copy-start.15 = (f32[16,16]{1,0:T(8,128)S(1)}, f32[16,16]{1,0:T(8,128)}, u32[]{:S(2)}) copy-start(f32[16,16]{1,0:T(8,128)} %param.17) | copy-start | bytes 3076
  158.9 4.2 %copy-start.16 = (f32[16]{0:T(128)S(1)}, f32[16]{0:T(128)}, u32[]{:S(2)}) copy-start(f32[16]{0:T(128)} %param.18) | copy-start | bytes 196
  158.9 4.1 %copy-start.17 = (f32[16]{0:T(128)S(1)}, f32[16]{0:T(128)}, u32[]{:S(2)}) copy-start(f32[16]{0:T(128)} %param.19) | copy-start | bytes 196
where the time goes:
time: 236 us; the launch traced here: 235 us
  matrix products  92 us (39%)
  waiting for transfers between devices  56.8 us (24%)
  other arithmetic  28.6 us (12%)
  starting transfers between devices  21.4 us (9%)
  local copies, waits for them, and re-layouts  17.5 us (7%)
  blocking collectives  15.5 us (7%)
    dot_general x16, matrix products, deposit_block(): jnp.einsum('shb,bl->shl', spread, low_hot, preferred_element_type=jnp.flo...  39 us
    ppermute x4, waiting for transfers between devices, padded_2(): after = lax.ppermute(initial, axis, down)  36.8 us
    dot_general x64, matrix products, react_block(): jnp.dot(prod_rate, concentration, precision=lax.Precision.HIGHEST)  26.8 us
    ppermute x4, waiting for transfers between devices, padded_2(): before = lax.ppermute(last, axis, up)  20 us
    dot_general x16, matrix products, react_block(): jnp.einsum('shl,bl->shb', coarse, low_hot, preferred_element_type=jnp.flo...  18.7 us
    all_to_all x1, blocking collectives, local(): lax.all_to_all(marked, ('lon', 'lat'), split_axis=0, concat_axis=0, tiled...  15.5 us
    add x16, other arithmetic, react_block(): blended = block_species + parcel_pull * (at_parcel - block_species)  14.9 us
    ppermute x4, starting transfers between devices, padded_2(): before = lax.ppermute(last, axis, up)  10.6 us
  transfers between devices with their start and end apart: 9, of which 6 were waited for; matrix products, arithmetic and copies ran while one was open for 27% of the time, Pallas kernels for 0%

commit v1 on v0

v1 whole, which is shorter than its diff:
```python
import functools

import jax
import jax.numpy as jnp
from jax import lax
from jax.experimental import pallas as pl
from jax.experimental.pallas import tpu as pltpu
from jax.sharding import PartitionSpec as P

ITERS = 4
LOW = 256
WINDOW = 8

grid_weight = 0.5
parcel_pull = 0.3

f32 = jnp.float32
bf16 = jnp.bfloat16
MESH = pl.DeviceIdType.MESH


def hot_rows(index_row, count):
    wide = jnp.broadcast_to(index_row.astype(f32), (16, index_row.shape[1])).astype(bf16)
    rows = lax.broadcasted_iota(jnp.int32, (16, index_row.shape[1]), 0).astype(f32).astype(bf16)
    one = jnp.ones_like(wide)
    zero = jnp.zeros_like(wide)
    return jnp.concatenate(
        [jnp.where(wide == rows + float(16 * g), one, zero) for g in range(count // 16)], axis=0
    )


def exchange_kernel(
    n_lon,
    n_lat,
    species_hbm,
    cells_ref,
    counts_ref,
    grid_ref,
    rate_ref,
    prod_ref,
    loss_ref,
    self_ref,
    arrived_out,
    cells_out,
    diffused_out,
    deposit_out,
    weight_hi_out,
    weight_lo_out,
    rates_out,
    arrived,
    marked,
    cells_in,
    field,
    east_halo,
    west_halo,
    north_halo,
    south_halo,
    edges,
    send_sem,
    recv_sem,
    send_cell_sem,
    recv_cell_sem,
    out_sem,
    out_cell_sem,
    halo_send,
    halo_recv,
):
    devices = n_lon * n_lat
    species_count = 16
    capacity = cells_ref.shape[1]
    lon = lax.axis_index("lon")
    lat = lax.axis_index("lat")
    me = lon * n_lat + lat

    def partner(step, sign):
        a = step // n_lat
        b = lax.rem(step, n_lat)
        to_lon = lax.rem(lon + sign * a + n_lon, n_lon)
        to_lat = lax.rem(lat + sign * b + n_lat, n_lat)
        return to_lon, to_lat, to_lon * n_lat + to_lat

    barrier = pltpu.get_barrier_semaphore()

    def greet(step, carry):
        to_lon, to_lat, _ = partner(step, 1)
        pl.semaphore_signal(barrier, inc=1, device_id=(to_lon, to_lat), device_id_type=MESH)
        return carry

    lax.fori_loop(1, devices, greet, 0)

    own = pltpu.make_async_copy(species_hbm.at[me], arrived.at[me], recv_sem.at[me])
    own.start()

    slot = lax.broadcasted_iota(jnp.int32, (1, capacity), 1)

    def mark(row, carry):
        marked[row] = jnp.where(slot < counts_ref[row], cells_ref[pl.ds(row, 1), :], -1)
        return carry

    lax.fori_loop(0, devices, mark, 0)
    pl.semaphore_wait(barrier, devices - 1)

    def species_copy(to_lon, to_lat, tile):
        return pltpu.make_async_remote_copy(
            src_ref=species_hbm.at[tile],
            dst_ref=arrived.at[me],
            send_sem=send_sem.at[tile],
            recv_sem=recv_sem.at[me],
            device_id=(to_lon, to_lat),
            device_id_type=MESH,
        )

    def cells_copy(to_lon, to_lat, tile):
        return pltpu.make_async_remote_copy(
            src_ref=marked.at[tile],
            dst_ref=cells_in.at[me],
            send_sem=send_cell_sem.at[tile],
            recv_sem=recv_cell_sem.at[me],
            device_id=(to_lon, to_lat),
            device_id_type=MESH,
        )

    def send(step):
        to_lon, to_lat, tile = partner(step, 1)
        cells_copy(to_lon, to_lat, tile).start()
        species_copy(to_lon, to_lat, tile).start()

    def send_step(step, carry):
        send(step)
        return carry

    for j in range(4):
        for level in range(8):
            field[0, j, level] = grid_ref[:, level, j, :]

    def halo_copies(turn):
        up_lon = lax.rem(lon + 1, n_lon)
        down_lon = lax.rem(lon + n_lon - 1, n_lon)
        up_lat = lax.rem(lat + 1, n_lat)
        down_lat = lax.rem(lat + n_lat - 1, n_lat)
        plan = (
            (field.at[turn, 0], east_halo.at[turn], (down_lon, lat)),
            (field.at[turn, 3], west_halo.at[turn], (up_lon, lat)),
            (edges.at[turn, 0], north_halo.at[turn], (lon, down_lat)),
            (edges.at[turn, 1], south_halo.at[turn], (lon, up_lat)),
        )
        return [
            pltpu.make_async_remote_copy(
                src_ref=source,
                dst_ref=target,
                send_sem=halo_send.at[turn, k],
                recv_sem=halo_recv.at[turn, k],
                device_id=device,
                device_id_type=MESH,
            )
            for k, (source, target, device) in enumerate(plan)
        ]

    def halo_start(turn):
        edges[turn] = jnp.zeros_like(edges[turn])
        for j in range(4):
            turned = field[turn, j].reshape(128, 128).T
            edges[turn, 0, j : j + 1, :] = turned[0:1, :]
            edges[turn, 1, j : j + 1, :] = turned[127:128, :]
        for copy in halo_copies(turn):
            copy.start()

    def column(row, lane_count):
        pick = lax.broadcasted_iota(jnp.int32, (16, 16), 0) == lax.broadcasted_iota(
            jnp.int32, (16, 16), 1
        )
        return jnp.broadcast_to(
            jnp.sum(jnp.where(pick, row, 0.0), axis=1, keepdims=True), (16, lane_count)
        )

    rate = column(rate_ref[...], 128)
    lane = lax.broadcasted_iota(jnp.int32, (128, 128), 1)

    def diffuse(turn, store):
        for copy in halo_copies(turn):
            copy.wait()
        north_cols = north_halo[turn].T
        south_cols = south_halo[turn].T
        for j in range(4):
            v = field[turn, j].reshape(128, 128)
            east = east_halo[turn] if j == 3 else field[turn, j + 1]
            west = west_halo[turn] if j == 0 else field[turn, j - 1]
            north_col = jnp.broadcast_to(north_cols[:, j : j + 1], (128, 128))
            south_col = jnp.broadcast_to(south_cols[:, j : j + 1], (128, 128))
            north_edge = jnp.where(lat == n_lat - 1, v, north_col)
            south_edge = jnp.where(lat == 0, v, south_col)
            north = jnp.where(lane == 127, north_edge, pltpu.roll(v, 127, 1))
            south = jnp.where(lane == 0, south_edge, pltpu.roll(v, 1, 1))
            above = jnp.concatenate([v[16:], v[112:]], axis=0)
            below = jnp.concatenate([v[:16], v[:112]], axis=0)
            laplace = (
                east.reshape(128, 128)
                + west.reshape(128, 128)
                + north
                + south
                + above
                + below
                - 6.0 * v
            )
            store(j, (v + jnp.concatenate([rate] * 8, axis=0) * laplace).reshape(8, 16, 128))

    def store_field(j, value):
        field[1, j] = value

    def store_out(j, value):
        diffused_out[j] = value

    def deposit(tile):
        cells = cells_in[tile]
        rounded = arrived[tile].astype(bf16)
        low_hot = hot_rows(lax.bitwise_and(cells, LOW - 1), LOW)
        high = jnp.broadcast_to(lax.shift_right_arithmetic(cells, 8).astype(f32), (16, capacity))
        high = high.astype(bf16)
        zero = jnp.zeros_like(rounded)
        rows = lax.broadcasted_iota(jnp.int32, (16, capacity), 0).astype(f32).astype(bf16)
        spread = jnp.concatenate(
            [jnp.where(high == float(h), rounded, zero) for h in range(16)]
            + [jnp.where(high == rows, jnp.ones_like(zero), zero)],
            axis=0,
        )
        deposit_out[...] += lax.dot_general(
            spread, low_hot, (((1,), (1,)), ((), ())), preferred_element_type=f32
        )

    def keep(tile):
        pltpu.make_async_copy(arrived.at[tile], arrived_out.at[tile], out_sem.at[tile]).start()
        pltpu.make_async_copy(cells_in.at[tile], cells_out.at[tile], out_cell_sem.at[tile]).start()

    def receive(step, carry):
        from_lon, from_lat, tile = partner(step, -1)
        pltpu.make_async_remote_copy(
            src_ref=marked.at[tile],
            dst_ref=cells_in.at[tile],
            send_sem=send_cell_sem.at[tile],
            recv_sem=recv_cell_sem.at[tile],
            device_id=(from_lon, from_lat),
            device_id_type=MESH,
        ).wait_recv()
        pltpu.make_async_remote_copy(
            src_ref=species_hbm.at[tile],
            dst_ref=arrived.at[tile],
            send_sem=send_sem.at[tile],
            recv_sem=recv_sem.at[tile],
            device_id=(from_lon, from_lat),
            device_id_type=MESH,
        ).wait_recv()
        keep(tile)
        deposit(tile)
        return carry

    def receive_send(step, carry):
        receive(step, carry)
        send(step + WINDOW)
        return carry

    halo_start(0)
    lax.fori_loop(1, WINDOW + 1, send_step, 0)

    spot = lax.broadcasted_iota(jnp.int32, (256, 16), 0)
    spots = lax.broadcasted_iota(jnp.int32, (256, 16), 1)
    tall = jnp.where(lax.rem(spot, 16) == spots, 1.0, 0.0).astype(bf16)
    prod = prod_ref[...]
    prod_hi = prod.astype(bf16)
    prod_lo = (prod - prod_hi.astype(f32)).astype(bf16)
    row_group = lax.broadcasted_iota(jnp.int32, (256, 256), 0) // 16
    col_group = lax.broadcasted_iota(jnp.int32, (256, 256), 1) // 16
    for part, target in ((prod_hi, weight_hi_out), (prod_lo, weight_lo_out)):
        half = jnp.dot(tall, part, preferred_element_type=f32).astype(bf16)
        full = lax.dot_general(half, tall, (((1,), (1,)), ((), ())), preferred_element_type=f32)
        target[...] = jnp.where(row_group == col_group, full, 0.0).astype(bf16)
    rates_out[0] = jnp.concatenate([column(loss_ref[...], 128)] * 16, axis=0)
    rates_out[1] = jnp.concatenate([column(self_ref[...], 128)] * 16, axis=0)

    deposit_out[...] = jnp.zeros_like(deposit_out)
    cells_in[me] = marked[me]
    own.wait()
    keep(me)
    deposit(me)

    first = devices // 4
    second = devices // 2
    lax.fori_loop(1, first, receive_send, 0)
    diffuse(0, store_field)
    halo_start(1)
    lax.fori_loop(first, second, receive_send, 0)
    diffuse(1, store_out)
    lax.fori_loop(second, devices - WINDOW, receive_send, 0)
    lax.fori_loop(devices - WINDOW, devices, receive, 0)

    def finish(step, carry):
        to_lon, to_lat, tile = partner(step, 1)
        cells_copy(to_lon, to_lat, tile).wait_send()
        species_copy(to_lon, to_lat, tile).wait_send()
        return carry

    lax.fori_loop(1, devices, finish, 0)

    def finish_keep(tile, carry):
        pltpu.make_async_copy(arrived.at[tile], arrived_out.at[tile], out_sem.at[tile]).wait()
        pltpu.make_async_copy(cells_in.at[tile], cells_out.at[tile], out_cell_sem.at[tile]).wait()
        return carry

    lax.fori_loop(0, devices, finish_keep, 0)


def react_kernel(
    arrived_ref,
    cells_ref,
    diffused_ref,
    deposit_ref,
    weight_hi_ref,
    weight_lo_ref,
    rates_ref,
    parcels_ref,
    mixed_ref,
    coarse,
):
    @pl.when((pl.program_id(0) == 0) & (pl.program_id(1) == 0))
    def mix():
        for h in range(16):
            for side in range(2):
                lanes = slice(128 * side, 128 * (side + 1))
                j = 2 * (h % 2) + side
                number = deposit_ref[256 + h : 257 + h, lanes]
                value = (
                    diffused_ref[j, h // 2]
                    + grid_weight * deposit_ref[16 * h : 16 * (h + 1), lanes]
                ) / (1.0 + grid_weight * number)
                mixed_ref[:, h // 2, j, :] = value
                coarse[16 * h : 16 * (h + 1), lanes] = value.astype(bf16)

    lanes = arrived_ref.shape[2]
    chunk = min(lanes, 256)
    grid_now = coarse[...]

    def react(turn, carry):
        where = pl.ds(pl.multiple_of(turn * chunk, chunk), chunk)
        parts = []
        for source in range(16):
            cells = cells_ref[source, :, where]
            low_hot = hot_rows(lax.bitwise_and(cells, LOW - 1), LOW)
            picked = jnp.dot(grid_now, low_hot, preferred_element_type=f32)
            high = jnp.broadcast_to(lax.shift_right_arithmetic(cells, 8), (16, chunk))
            at_parcel = picked[:16]
            for h in range(1, 16):
                at_parcel = jnp.where(high == h, picked[16 * h : 16 * (h + 1)], at_parcel)
            start = arrived_ref[source, :, where]
            parts.append(start + parcel_pull * (at_parcel - start))
        blended = jnp.concatenate(parts, axis=0)
        state = blended
        loss = jnp.concatenate([rates_ref[0]] * (chunk // 128), axis=1)
        self_loss = jnp.concatenate([rates_ref[1]] * (chunk // 128), axis=1)
        for sweep in range(ITERS):
            high_part = state.astype(bf16)
            low_part = (state - high_part.astype(f32)).astype(bf16)
            produced = (
                blended
                + jnp.dot(weight_hi_ref[...], high_part, preferred_element_type=f32)
                + jnp.dot(weight_hi_ref[...], low_part, preferred_element_type=f32)
                + jnp.dot(weight_lo_ref[...], high_part, preferred_element_type=f32)
            )
            state = produced / (1.0 + loss + self_loss * state)
        for source in range(16):
            alive = jnp.broadcast_to(cells_ref[source, :, where] >= 0, (16, chunk))
            parcels_ref[source, :, where] = jnp.where(
                alive, state[16 * source : 16 * (source + 1)], 0.0
            )
        return carry

    lax.fori_loop(0, lanes // chunk, react, 0)


def local(
    send_species, send_cells, send_counts, grid_state, diff_rate, prod_rate, loss_rate, self_rate
):
    n_lon = lax.axis_size("lon")
    n_lat = lax.axis_size("lat")
    devices, species_count, capacity = send_species.shape
    vmem = pl.BlockSpec(memory_space=pltpu.VMEM)
    hbm = pl.BlockSpec(memory_space=pl.ANY)
    arrived, cells, diffused, deposit, weight_hi, weight_lo, rates = pl.pallas_call(
        functools.partial(exchange_kernel, n_lon, n_lat),
        out_shape=(
            jax.ShapeDtypeStruct((devices, species_count, capacity), f32),
            jax.ShapeDtypeStruct((devices, 1, capacity), jnp.int32),
            jax.ShapeDtypeStruct((4, 8, 16, 128), f32),
            jax.ShapeDtypeStruct((272, LOW), f32),
            jax.ShapeDtypeStruct((256, 256), bf16),
            jax.ShapeDtypeStruct((256, 256), bf16),
            jax.ShapeDtypeStruct((2, 256, 128), f32),
        ),
        in_specs=[
            hbm,
            vmem,
            pl.BlockSpec(memory_space=pltpu.SMEM),
            vmem,
            vmem,
            vmem,
            vmem,
            vmem,
        ],
        out_specs=(hbm, hbm, vmem, vmem, vmem, vmem, vmem),
        scratch_shapes=[
            pltpu.VMEM((devices, species_count, capacity), f32),
            pltpu.VMEM((devices, 1, capacity), jnp.int32),
            pltpu.VMEM((devices, 1, capacity), jnp.int32),
            pltpu.VMEM((2, 4, 8, 16, 128), f32),
            pltpu.VMEM((2, 8, 16, 128), f32),
            pltpu.VMEM((2, 8, 16, 128), f32),
            pltpu.VMEM((2, 8, 128), f32),
            pltpu.VMEM((2, 8, 128), f32),
            pltpu.VMEM((2, 2, 8, 128), f32),
            pltpu.SemaphoreType.DMA((devices,)),
            pltpu.SemaphoreType.DMA((devices,)),
            pltpu.SemaphoreType.DMA((devices,)),
            pltpu.SemaphoreType.DMA((devices,)),
            pltpu.SemaphoreType.DMA((devices,)),
            pltpu.SemaphoreType.DMA((devices,)),
            pltpu.SemaphoreType.DMA((2, 4)),
            pltpu.SemaphoreType.DMA((2, 4)),
        ],
        compiler_params=pltpu.CompilerParams(
            collective_id=0, has_side_effects=True, vmem_limit_bytes=40 * 1024 * 1024
        ),
        name="exchange",
    )(
        send_species,
        send_cells,
        send_counts,
        grid_state,
        diff_rate.reshape(1, 16),
        prod_rate,
        loss_rate.reshape(1, 16),
        self_rate.reshape(1, 16),
    )

    lanes = min(capacity, 512)
    whole = lambda shape: pl.BlockSpec(shape, lambda g, k: (0,) * len(shape))
    return pl.pallas_call(
        react_kernel,
        grid=(devices // 16, capacity // lanes),
        out_shape=(
            jax.ShapeDtypeStruct(send_species.shape, f32),
            jax.ShapeDtypeStruct(grid_state.shape, f32),
        ),
        in_specs=[
            pl.BlockSpec((16, 16, lanes), lambda g, k: (g, 0, k)),
            pl.BlockSpec((16, 1, lanes), lambda g, k: (g, 0, k)),
            whole((4, 8, 16, 128)),
            whole((272, LOW)),
            whole((256, 256)),
            whole((256, 256)),
            whole((2, 256, 128)),
        ],
        out_specs=(
            pl.BlockSpec((16, 16, lanes), lambda g, k: (g, 0, k)),
            whole(grid_state.shape),
        ),
        scratch_shapes=[pltpu.VMEM((256, LOW), bf16)],
        compiler_params=pltpu.CompilerParams(vmem_limit_bytes=40 * 1024 * 1024),
        name="react",
    )(arrived, cells, diffused, deposit, weight_hi, weight_lo, rates)


def solution(mesh):
    placed = (
        P(("lon", "lat"), None, None),
        P(("lon", "lat"), None),
        P(("lon", "lat")),
        P(None, None, "lon", "lat"),
        P(),
        P(),
        P(),
        P(),
    )
    return jax.shard_map(
        local,
        mesh=mesh,
        in_specs=placed,
        out_specs=(P(("lon", "lat"), None, None), P(None, None, "lon", "lat")),
        check_vma=False,
    )
```

time: 236 us -> 85.5 us (0.36)
  matrix products: 92 us -> 0 us
  Pallas kernels: 0 us -> 77.3 us
  waiting for transfers between devices: 56.8 us -> 0 us
  other arithmetic: 28.6 us -> 0 us
  starting transfers between devices: 21.4 us -> 0 us
  blocking collectives: 15.5 us -> 0 us
  local copies, waits for them, and re-layouts: 17.5 us -> 6.75 us
    dot_general x112 -> x0, matrix products: 92 us -> none  [the longest x16 39 us: deposit_block(): jnp.einsum('shb,bl->shl', spread, low_hot, preferred_element_type=jnp.flo...]
    pallas_call x0 -> x2, Pallas kernels: none -> 77.3 us  [the longest x1 59.5 us: local(): pl.pallas_call(functools.partial(exchange_kernel, n_lon, n_lat), out_shap...]
    ppermute x8 -> x0, waiting for transfers between devices: 56.8 us -> none  [the longest x4 36.8 us: padded_2(): after = lax.ppermute(initial, axis, down)]
    ppermute x8 -> x0, starting transfers between devices: 18.5 us -> none  [the longest x4 10.6 us: padded_2(): before = lax.ppermute(last, axis, up)]
    add x34 -> x0, other arithmetic: 17.2 us -> none  [the longest x16 14.9 us: react_block(): blended = block_species + parcel_pull * (at_parcel - block_species)]
    all_to_all x1 -> x0, blocking collectives: 15.5 us -> none  [local(): lax.all_to_all(marked, ('lon', 'lat'), split_axis=0, concat_axis=0, tiled...]
    transpose x2 -> x0, local copies, waits for them, and re-layouts: 5.38 us -> none  [the longest x1 2.81 us: local(): reacted.transpose(1, 0, 2)]
    slice x8 -> x0, local copies, waits for them, and re-layouts: 4.06 us -> none  [the longest x2 2.27 us: padded_2(): initial = lax.slice_in_dim(x, 0, width, axis=dim)]
  transfers between devices with their start and end apart: 9 -> 0, of which waited for: 6 -> 0; matrix products, arithmetic and copies ran while one was open for 27% -> 0% of each run, Pallas kernels for 0% -> 0%
where the time goes in v1:
time: 85.5 us; the launch traced here: 84.7 us
  Pallas kernels  77.3 us (90%)
  local copies, waits for them, and re-layouts  6.75 us (8%)
    pallas_call x1, Pallas kernels, local(): pl.pallas_call(functools.partial(exchange_kernel, n_lon, n_lat), out_shap...  59.5 us
    pallas_call x1, Pallas kernels, local(): pl.pallas_call(react_kernel, grid=(devices // 16, capacity // lanes), out...  17.8 us
    unnamed x16, local copies, waits for them, and re-layouts  6.75 us

profile of v1, /device:TPU:0, one launch (start us, length us, event | category | flops | bytes accessed | tf_op | source)
XLA Modules:
  0.0 84.7 jit_solution(4359907408338471937)
XLA Ops:
  0.6 0.0 copy-start
  0.6 1.6 %copy-done = f32[32,16,1024]{2,1,0:T(8,128)S(1)} copy-done((f32[32,16,1024]{2,1,0:T(8,128)S(1)}, f32[32,16,1024]{2,1,0:T(8,128)}, u32[]{:S(2)}) %copy-start) | copy-done | bytes 2097176
  2.2 0.0 copy-start.1
  2.2 0.9 %copy-done.1 = f32[16,8,4,128]{3,2,1,0:T(4,128)S(1)} copy-done((f32[16,8,4,128]{3,2,1,0:T(4,128)S(1)}, f32[16,8,4,128]{3,2,1,0:T(4,128)}, u32[]{:S(2)}) %copy-start.1) | copy-done | bytes 262168
  3.2 0.0 copy-start.2
  3.2 0.9 %copy-done.2 = s32[32,1024]{1,0:T(8,128)S(1)} copy-done((s32[32,1024]{1,0:T(8,128)S(1)}, s32[32,1024]{1,0:T(8,128)}, u32[]{:S(2)}) %copy-start.2) | copy-done | bytes 131096
  4.1 0.0 copy-start.3
  4.1 0.7 copy-done.3
  4.8 0.0 copy-start.4
  4.8 0.7 copy-done.4
  5.4 0.0 copy-start.5
  5.4 0.7 copy-done.5
  6.1 0.0 copy-start.6
  6.1 0.7 copy-done.6
  6.7 0.0 copy-start.7
  6.7 0.7 copy-done.7
  7.4 59.5 %exchange.1 = (f32[32,16,1024]{2,1,0:T(8,128)S(1)}, s32[32,1,1024]{2,1,0:T(1,128)S(1)}, f32[4,8,16,128]{3,2,1,0:T(8,128)S(1)}, f32[272,256]{1,0:T(8,128)S(1)}, b...) custom-call(f32[32,16,1024]{2,1,0:T(8,128)S(1)} %copy-done, ...), custom_call_target="tpu_custom_call" | custom-call | tf_op jit(solution)/shard_map/exchange/pallas_call | solution.py:386
  67.0 17.8 %react.1 = (f32[32,16,1024]{2,1,0:T(8,128)}, f32[16,8,4,128]{3,2,1,0:T(4,128)}) custom-call(f32[32,16,1024]{2,1,0:T(8,128)S(1)} %get-tuple-element.9.arrived_ref, s32[32,1,1024]{2,1,0:T(1,128)S(1)} %get-tuple-element.10.cells_ref, f32[4,8,16,128]{3,2,1,0:T(8,128)S(1)} %get-tuple-element.11.diffused_ref, f32[272,256]{1,0:T(8,128)S(1)} %get-tuple-element.12.deposit_ref, ...), custom_call_target="tpu_custom_call" | custom-call | tf_op jit(solution)/shard_map/react/pallas_call | solution.py:444
Async XLA Ops:
  0.6 1.6 %copy-start = (f32[32,16,1024]{2,1,0:T(8,128)S(1)}, f32[32,16,1024]{2,1,0:T(8,128)}, u32[]{:S(2)}) copy-start(f32[32,16,1024]{2,1,0:T(8,128)} %species_hbm.1) | copy-start | bytes 6291460
  2.2 0.9 %copy-start.1 = (f32[16,8,4,128]{3,2,1,0:T(4,128)S(1)}, f32[16,8,4,128]{3,2,1,0:T(4,128)}, u32[]{:S(2)}) copy-start(f32[16,8,4,128]{3,2,1,0:T(4,128)} %grid_ref.1) | copy-start | bytes 786436
  3.2 0.9 %copy-start.2 = (s32[32,1024]{1,0:T(8,128)S(1)}, s32[32,1024]{1,0:T(8,128)}, u32[]{:S(2)}) copy-start(s32[32,1024]{1,0:T(8,128)} %cells_ref.1) | copy-start | bytes 393220
  4.1 0.7 copy-start.3
  4.8 0.7 copy-start.4
  5.4 0.7 copy-start.5
  6.1 0.7 copy-start.6
  6.7 0.7 copy-start.7

commit v2 on v1

--- a/solution.py
+++ b/solution.py
@@ -9,7 +9,7 @@
 
 ITERS = 4
 LOW = 256
-WINDOW = 8
+WINDOW = 16
 
 grid_weight = 0.5
 parcel_pull = 0.3
@@ -33,6 +33,19 @@
     n_lon,
     n_lat,
     species_hbm,
+    cells_hbm,
+    counts_hbm,
+    grid_hbm,
+    rate_hbm,
+    prod_hbm,
+    loss_hbm,
+    self_hbm,
+    arrived_out,
+    cells_out,
+    diffused_out,
+    deposit_out,
+    weight_out,
+    rates_out,
     cells_ref,
     counts_ref,
     grid_ref,
@@ -40,13 +53,7 @@
     prod_ref,
     loss_ref,
     self_ref,
-    arrived_out,
-    cells_out,
-    diffused_out,
-    deposit_out,
-    weight_hi_out,
-    weight_lo_out,
-    rates_out,
+    load_sem,
     arrived,
     marked,
     cells_in,
@@ -79,6 +86,22 @@
         to_lat = lax.rem(lat + sign * b + n_lat, n_lat)
         return to_lon, to_lat, to_lon * n_lat + to_lat
 
+    loads = [
+        pltpu.make_async_copy(source, target, load_sem.at[k])
+        for k, (source, target) in enumerate(
+            (
+                (cells_hbm, cells_ref),
+                (counts_hbm, counts_ref),
+                (grid_hbm, grid_ref),
+                (rate_hbm, rate_ref),
+                (prod_hbm, prod_ref),
+                (loss_hbm, loss_ref),
+                (self_hbm, self_ref),
+            )
+        )
+    ]
+    for load in loads:
+        load.start()
     barrier = pltpu.get_barrier_semaphore()
 
     def greet(step, carry):
@@ -91,6 +114,8 @@
     own = pltpu.make_async_copy(species_hbm.at[me], arrived.at[me], recv_sem.at[me])
     own.start()
 
+    loads[0].wait()
+    loads[1].wait()
     slot = lax.broadcasted_iota(jnp.int32, (1, capacity), 1)
 
     def mark(row, carry):
@@ -128,6 +153,10 @@
     def send_step(step, carry):
         send(step)
         return carry
+
+    lax.fori_loop(1, WINDOW + 1, send_step, 0)
+    for load in loads[2:]:
+        load.wait()
 
     for j in range(4):
         for level in range(8):
@@ -259,7 +288,6 @@
         return carry
 
     halo_start(0)
-    lax.fori_loop(1, WINDOW + 1, send_step, 0)
 
     spot = lax.broadcasted_iota(jnp.int32, (256, 16), 0)
     spots = lax.broadcasted_iota(jnp.int32, (256, 16), 1)
@@ -267,14 +295,20 @@
     prod = prod_ref[...]
     prod_hi = prod.astype(bf16)
     prod_lo = (prod - prod_hi.astype(f32)).astype(bf16)
-    row_group = lax.broadcasted_iota(jnp.int32, (256, 256), 0) // 16
-    col_group = lax.broadcasted_iota(jnp.int32, (256, 256), 1) // 16
-    for part, target in ((prod_hi, weight_hi_out), (prod_lo, weight_lo_out)):
+    row = lax.broadcasted_iota(jnp.int32, (256, 256), 0)
+    col = lax.broadcasted_iota(jnp.int32, (256, 256), 1)
+    same = lax.rem(row // 16, 8) == lax.rem(col // 16, 8)
+    wide = []
+    for part in (prod_hi, prod_lo):
         half = jnp.dot(tall, part, preferred_element_type=f32).astype(bf16)
-        full = lax.dot_general(half, tall, (((1,), (1,)), ((), ())), preferred_element_type=f32)
-        target[...] = jnp.where(row_group == col_group, full, 0.0).astype(bf16)
-    rates_out[0] = jnp.concatenate([column(loss_ref[...], 128)] * 16, axis=0)
-    rates_out[1] = jnp.concatenate([column(self_ref[...], 128)] * 16, axis=0)
+        wide.append(
+            lax.dot_general(half, tall, (((1,), (1,)), ((), ())), preferred_element_type=f32)
+        )
+    weight_out[...] = jnp.where(
+        same, jnp.where(row < 128, wide[0], jnp.where(col < 128, wide[1], 0.0)), 0.0
+    ).astype(bf16)
+    rates_out[0] = jnp.concatenate([1.0 + column(loss_ref[...], 128)] * 8, axis=0)
+    rates_out[1] = jnp.concatenate([column(self_ref[...], 128)] * 8, axis=0)
 
     deposit_out[...] = jnp.zeros_like(deposit_out)
     cells_in[me] = marked[me]
@@ -313,8 +347,7 @@
     cells_ref,
     diffused_ref,
     deposit_ref,
-    weight_hi_ref,
-    weight_lo_ref,
+    weight_ref,
     rates_ref,
     parcels_ref,
     mixed_ref,
@@ -337,42 +370,47 @@
     lanes = arrived_ref.shape[2]
     chunk = min(lanes, 256)
     grid_now = coarse[...]
-
-    def react(turn, carry):
-        where = pl.ds(pl.multiple_of(turn * chunk, chunk), chunk)
-        parts = []
-        for source in range(16):
-            cells = cells_ref[source, :, where]
-            low_hot = hot_rows(lax.bitwise_and(cells, LOW - 1), LOW)
-            picked = jnp.dot(grid_now, low_hot, preferred_element_type=f32)
-            high = jnp.broadcast_to(lax.shift_right_arithmetic(cells, 8), (16, chunk))
-            at_parcel = picked[:16]
-            for h in range(1, 16):
-                at_parcel = jnp.where(high == h, picked[16 * h : 16 * (h + 1)], at_parcel)
-            start = arrived_ref[source, :, where]
-            parts.append(start + parcel_pull * (at_parcel - start))
-        blended = jnp.concatenate(parts, axis=0)
-        state = blended
-        loss = jnp.concatenate([rates_ref[0]] * (chunk // 128), axis=1)
-        self_loss = jnp.concatenate([rates_ref[1]] * (chunk // 128), axis=1)
-        for sweep in range(ITERS):
-            high_part = state.astype(bf16)
-            low_part = (state - high_part.astype(f32)).astype(bf16)
-            produced = (
-                blended
-                + jnp.dot(weight_hi_ref[...], high_part, preferred_element_type=f32)
-                + jnp.dot(weight_hi_ref[...], low_part, preferred_element_type=f32)
-                + jnp.dot(weight_lo_ref[...], high_part, preferred_element_type=f32)
+    loss = jnp.concatenate([rates_ref[0]] * (chunk // 128), axis=1)
+    self_loss = jnp.concatenate([rates_ref[1]] * (chunk // 128), axis=1)
+
+    def blend(source, where):
+        cells = cells_ref[source, :, where]
+        low_hot = hot_rows(lax.bitwise_and(cells, LOW - 1), LOW)
+        picked = jnp.dot(grid_now, low_hot, preferred_element_type=f32)
+        found = [picked[16 * h : 16 * (h + 1)] for h in range(16)]
+        for bit in range(4):
+            is_set = lax.bitwise_and(cells, LOW << bit) != 0
+            is_set = jnp.broadcast_to(is_set, (16, chunk))
+            found = [
+                jnp.where(is_set, found[2 * k + 1], found[2 * k]) for k in range(len(found) // 2)
+            ]
+        start = arrived_ref[source, :, where]
+        return start + parcel_pull * (found[0] - start)
+
+    for turn in range(lanes // chunk):
+        where = slice(chunk * turn, chunk * (turn + 1))
+        for first in range(0, 16, 8):
+            blended = jnp.concatenate(
+                [blend(source, where) for source in range(first, first + 8)], axis=0
             )
-            state = produced / (1.0 + loss + self_loss * state)
-        for source in range(16):
-            alive = jnp.broadcast_to(cells_ref[source, :, where] >= 0, (16, chunk))
-            parcels_ref[source, :, where] = jnp.where(
-                alive, state[16 * source : 16 * (source + 1)], 0.0
-            )
-        return carry
-
-    lax.fori_loop(0, lanes // chunk, react, 0)
+            state = blended
+            for sweep in range(ITERS):
+                high_part = state.astype(bf16)
+                low_part = (state - high_part.astype(f32)).astype(bf16)
+                product = jnp.dot(
+                    weight_ref[...],
+                    jnp.concatenate([high_part, low_part], axis=0),
+                    preferred_element_type=f32,
+                )
+                produced = blended + (product[:128] + product[128:])
+                bottom = loss + self_loss * state
+                inverse = pl.reciprocal(bottom, approx=True)
+                state = produced * (inverse * (2.0 - bottom * inverse))
+            for k in range(8):
+                alive = jnp.broadcast_to(cells_ref[first + k, :, where] >= 0, (16, chunk))
+                parcels_ref[first + k, :, where] = jnp.where(
+                    alive, state[16 * k : 16 * (k + 1)], 0.0
+                )
 
 
 def local(
@@ -383,7 +421,7 @@
     devices, species_count, capacity = send_species.shape
     vmem = pl.BlockSpec(memory_space=pltpu.VMEM)
     hbm = pl.BlockSpec(memory_space=pl.ANY)
-    arrived, cells, diffused, deposit, weight_hi, weight_lo, rates = pl.pallas_call(
+    arrived, cells, diffused, deposit, weight, rates = pl.pallas_call(
         functools.partial(exchange_kernel, n_lon, n_lat),
         out_shape=(
             jax.ShapeDtypeStruct((devices, species_count, capacity), f32),
@@ -391,21 +429,19 @@
             jax.ShapeDtypeStruct((4, 8, 16, 128), f32),
             jax.ShapeDtypeStruct((272, LOW), f32),
             jax.ShapeDtypeStruct((256, 256), bf16),
-            jax.ShapeDtypeStruct((256, 256), bf16),
-            jax.ShapeDtypeStruct((2, 256, 128), f32),
+            jax.ShapeDtypeStruct((2, 128, 128), f32),
         ),
-        in_specs=[
-            hbm,
-            vmem,
-            pl.BlockSpec(memory_space=pltpu.SMEM),
-            vmem,
-            vmem,
-            vmem,
-            vmem,
-            vmem,
-        ],
-        out_specs=(hbm, hbm, vmem, vmem, vmem, vmem, vmem),
+        in_specs=[pl.BlockSpec(memory_space=pltpu.HBM)] * 8,
+        out_specs=(hbm, hbm, vmem, vmem, vmem, vmem),
         scratch_shapes=[
+            pltpu.VMEM(send_cells.shape, jnp.int32),
+            pltpu.SMEM(send_counts.shape, jnp.int32),
+            pltpu.VMEM(grid_state.shape, f32),
+            pltpu.VMEM((1, 16), f32),
+            pltpu.VMEM((16, 16), f32),
+            pltpu.VMEM((1, 16), f32),
+            pltpu.VMEM((1, 16), f32),
+            pltpu.SemaphoreType.DMA((7,)),
             pltpu.VMEM((devices, species_count, capacity), f32),
             pltpu.VMEM((devices, 1, capacity), jnp.int32),
             pltpu.VMEM((devices, 1, capacity), jnp.int32),
@@ -454,8 +490,7 @@
             whole((4, 8, 16, 128)),
             whole((272, LOW)),
             whole((256, 256)),
-            whole((256, 256)),
-            whole((2, 256, 128)),
+            whole((2, 128, 128)),
         ],
         out_specs=(
             pl.BlockSpec((16, 16, lanes), lambda g, k: (g, 0, k)),
@@ -464,7 +499,7 @@
         scratch_shapes=[pltpu.VMEM((256, LOW), bf16)],
         compiler_params=pltpu.CompilerParams(vmem_limit_bytes=40 * 1024 * 1024),
         name="react",
-    )(arrived, cells, diffused, deposit, weight_hi, weight_lo, rates)
+    )(arrived, cells, diffused, deposit, weight, rates)
 
 
 def solution(mesh):

time: 85.5 us -> 87 us (1.018)
  Pallas kernels: 77.3 us -> 78.9 us
    pallas_call x1, Pallas kernels: 17.8 us -> 19.7 us  [local(): pl.pallas_call(react_kernel, grid=(devices // 16, capacity // lanes), out...]
where the time goes in v2:
time: 87 us; the launch traced here: 86.3 us
  Pallas kernels  78.9 us (91%)
  local copies, waits for them, and re-layouts  6.75 us (8%)
    pallas_call x1, Pallas kernels, local(): pl.pallas_call(functools.partial(exchange_kernel, n_lon, n_lat), out_shap...  59.2 us
    pallas_call x1, Pallas kernels, local(): pl.pallas_call(react_kernel, grid=(devices // 16, capacity // lanes), out...  19.7 us
    unnamed x16, local copies, waits for them, and re-layouts  6.75 us

profile of v2, /device:TPU:0, one launch (start us, length us, event | category | flops | bytes accessed | tf_op | source)
XLA Modules:
  0.0 86.3 jit_solution(8497074312622294025)
XLA Ops:
  0.6 0.0 copy-start
  0.6 1.6 %copy-done = f32[32,16,1024]{2,1,0:T(8,128)S(1)} copy-done((f32[32,16,1024]{2,1,0:T(8,128)S(1)}, f32[32,16,1024]{2,1,0:T(8,128)}, u32[]{:S(2)}) %copy-start) | copy-done | bytes 2097176
  2.2 0.0 copy-start.1
  2.2 0.9 %copy-done.1 = f32[16,8,4,128]{3,2,1,0:T(4,128)S(1)} copy-done((f32[16,8,4,128]{3,2,1,0:T(4,128)S(1)}, f32[16,8,4,128]{3,2,1,0:T(4,128)}, u32[]{:S(2)}) %copy-start.1) | copy-done | bytes 262168
  3.2 0.0 copy-start.2
  3.2 0.9 %copy-done.2 = s32[32,1024]{1,0:T(8,128)S(1)} copy-done((s32[32,1024]{1,0:T(8,128)S(1)}, s32[32,1024]{1,0:T(8,128)}, u32[]{:S(2)}) %copy-start.2) | copy-done | bytes 131096
  4.1 0.0 copy-start.3
  4.1 0.7 copy-done.3
  4.8 0.0 copy-start.4
  4.8 0.7 copy-done.4
  5.4 0.0 copy-start.5
  5.4 0.7 copy-done.5
  6.1 0.0 copy-start.6
  6.1 0.7 copy-done.6
  6.7 0.0 copy-start.7
  6.7 0.7 copy-done.7
  7.4 59.2 %exchange.1 = (f32[32,16,1024]{2,1,0:T(8,128)S(1)}, s32[32,1,1024]{2,1,0:T(1,128)S(1)}, f32[4,8,16,128]{3,2,1,0:T(8,128)S(1)}, f32[272,256]{1,0:T(8,128)S(1)}, b...) custom-call(f32[32,16,1024]{2,1,0:T(8,128)S(1)} %copy-done, s32[32,1024]{1,0:T(8,128)S(1)} %copy-done.2, ...), custom_call_target="tpu_custom_call" | custom-call | tf_op jit(solution)/shard_map/exchange/pallas_call | solution.py:424
  66.6 19.7 %react.1 = (f32[32,16,1024]{2,1,0:T(8,128)}, f32[16,8,4,128]{3,2,1,0:T(4,128)}) custom-call(f32[32,16,1024]{2,1,0:T(8,128)S(1)} %get-tuple-element.8.arrived_ref, s32[32,1,1024]{2,1,0:T(1,128)S(1)} %get-tuple-element.9.cells_ref, f32[4,8,16,128]{3,2,1,0:T(8,128)S(1)} %get-tuple-element.10.diffused_ref, f32[272,256]{1,0:T(8,128)S(1)} %get-tuple-element.11.deposit_ref, ...), custom_call_target="tpu_custom_call" | custom-call | tf_op jit(solution)/shard_map/react/pallas_call | solution.py:480
Async XLA Ops:
  0.6 1.6 %copy-start = (f32[32,16,1024]{2,1,0:T(8,128)S(1)}, f32[32,16,1024]{2,1,0:T(8,128)}, u32[]{:S(2)}) copy-start(f32[32,16,1024]{2,1,0:T(8,128)} %species_hbm.1) | copy-start | bytes 6291460
  2.2 0.9 %copy-start.1 = (f32[16,8,4,128]{3,2,1,0:T(4,128)S(1)}, f32[16,8,4,128]{3,2,1,0:T(4,128)}, u32[]{:S(2)}) copy-start(f32[16,8,4,128]{3,2,1,0:T(4,128)} %grid_hbm.1) | copy-start | bytes 786436
  3.2 0.9 %copy-start.2 = (s32[32,1024]{1,0:T(8,128)S(1)}, s32[32,1024]{1,0:T(8,128)}, u32[]{:S(2)}) copy-start(s32[32,1024]{1,0:T(8,128)} %cells_hbm.1) | copy-start | bytes 393220
  4.1 0.7 copy-start.3
  4.8 0.7 copy-start.4
  5.4 0.7 copy-start.5
  6.1 0.7 copy-start.6
  6.7 0.7 copy-start.7

commit v3 on v2

--- a/solution.py
+++ b/solution.py
@@ -9,7 +9,8 @@
 
 ITERS = 4
 LOW = 256
-WINDOW = 16
+WINDOW = 31
+VMEM_BYTES = 62 * 1024 * 1024
 
 grid_weight = 0.5
 parcel_pull = 0.3
@@ -284,7 +285,11 @@
 
     def receive_send(step, carry):
         receive(step, carry)
-        send(step + WINDOW)
+
+        @pl.when(step + WINDOW < devices)
+        def refill():
+            send(step + WINDOW)
+
         return carry
 
     halo_start(0)
@@ -323,8 +328,7 @@
     halo_start(1)
     lax.fori_loop(first, second, receive_send, 0)
     diffuse(1, store_out)
-    lax.fori_loop(second, devices - WINDOW, receive_send, 0)
-    lax.fori_loop(devices - WINDOW, devices, receive, 0)
+    lax.fori_loop(second, devices, receive_send, 0)
 
     def finish(step, carry):
         to_lon, to_lat, tile = partner(step, 1)
@@ -352,6 +356,7 @@
     parcels_ref,
     mixed_ref,
     coarse,
+    blended,
 ):
     @pl.when((pl.program_id(0) == 0) & (pl.program_id(1) == 0))
     def mix():
@@ -369,48 +374,50 @@
 
     lanes = arrived_ref.shape[2]
     chunk = min(lanes, 256)
-    grid_now = coarse[...]
+    chunks = [slice(k, k + chunk) for k in range(0, lanes, chunk)]
     loss = jnp.concatenate([rates_ref[0]] * (chunk // 128), axis=1)
     self_loss = jnp.concatenate([rates_ref[1]] * (chunk // 128), axis=1)
 
-    def blend(source, where):
-        cells = cells_ref[source, :, where]
-        low_hot = hot_rows(lax.bitwise_and(cells, LOW - 1), LOW)
-        picked = jnp.dot(grid_now, low_hot, preferred_element_type=f32)
-        found = [picked[16 * h : 16 * (h + 1)] for h in range(16)]
-        for bit in range(4):
-            is_set = lax.bitwise_and(cells, LOW << bit) != 0
-            is_set = jnp.broadcast_to(is_set, (16, chunk))
-            found = [
-                jnp.where(is_set, found[2 * k + 1], found[2 * k]) for k in range(len(found) // 2)
-            ]
-        start = arrived_ref[source, :, where]
-        return start + parcel_pull * (found[0] - start)
-
-    for turn in range(lanes // chunk):
-        where = slice(chunk * turn, chunk * (turn + 1))
-        for first in range(0, 16, 8):
-            blended = jnp.concatenate(
-                [blend(source, where) for source in range(first, first + 8)], axis=0
+    def blend(source, carry):
+        for where in chunks:
+            cells = cells_ref[source, :, where]
+            low_hot = hot_rows(lax.bitwise_and(cells, LOW - 1), LOW)
+            picked = jnp.dot(coarse[...], low_hot, preferred_element_type=f32)
+            high = jnp.broadcast_to(lax.shift_right_arithmetic(cells, 8), (16, chunk))
+            found = picked[:16]
+            for h in range(1, 16):
+                found = jnp.where(high == h, picked[16 * h : 16 * (h + 1)], found)
+            start = arrived_ref[source, :, where]
+            blended[source, :, where] = start + parcel_pull * (found - start)
+        return carry
+
+    lax.fori_loop(0, 16, blend, 0, unroll=2)
+
+    groups = [(first, where) for where in chunks for first in (0, 8)]
+    starts = [
+        blended[first : first + 8, :, where].reshape(128, chunk) for first, where in groups
+    ]
+    states = starts
+    for sweep in range(ITERS):
+        parts = []
+        for state in states:
+            high_part = state.astype(bf16)
+            low_part = (state - high_part.astype(f32)).astype(bf16)
+            parts.append(jnp.concatenate([high_part, low_part], axis=0))
+        products = [jnp.dot(weight_ref[...], part, preferred_element_type=f32) for part in parts]
+        later = []
+        for start, state, product in zip(starts, states, products):
+            produced = start + (product[:128] + product[128:])
+            bottom = loss + self_loss * state
+            inverse = pl.reciprocal(bottom, approx=True)
+            later.append(produced * (inverse * (2.0 - bottom * inverse)))
+        states = later
+    for (first, where), state in zip(groups, states):
+        for k in range(8):
+            alive = jnp.broadcast_to(cells_ref[first + k, :, where] >= 0, (16, chunk))
+            parcels_ref[first + k, :, where] = jnp.where(
+                alive, state[16 * k : 16 * (k + 1)], 0.0
             )
-            state = blended
-            for sweep in range(ITERS):
-                high_part = state.astype(bf16)
-                low_part = (state - high_part.astype(f32)).astype(bf16)
-                product = jnp.dot(
-                    weight_ref[...],
-                    jnp.concatenate([high_part, low_part], axis=0),
-                    preferred_element_type=f32,
-                )
-                produced = blended + (product[:128] + product[128:])
-                bottom = loss + self_loss * state
-                inverse = pl.reciprocal(bottom, approx=True)
-                state = produced * (inverse * (2.0 - bottom * inverse))
-            for k in range(8):
-                alive = jnp.broadcast_to(cells_ref[first + k, :, where] >= 0, (16, chunk))
-                parcels_ref[first + k, :, where] = jnp.where(
-                    alive, state[16 * k : 16 * (k + 1)], 0.0
-                )
 
 
 def local(
@@ -461,7 +468,7 @@
             pltpu.SemaphoreType.DMA((2, 4)),
         ],
         compiler_params=pltpu.CompilerParams(
-            collective_id=0, has_side_effects=True, vmem_limit_bytes=40 * 1024 * 1024
+            collective_id=0, has_side_effects=True, vmem_limit_bytes=VMEM_BYTES
         ),
         name="exchange",
     )(
@@ -496,8 +503,8 @@
             pl.BlockSpec((16, 16, lanes), lambda g, k: (g, 0, k)),
             whole(grid_state.shape),
         ),
-        scratch_shapes=[pltpu.VMEM((256, LOW), bf16)],
-        compiler_params=pltpu.CompilerParams(vmem_limit_bytes=40 * 1024 * 1024),
+        scratch_shapes=[pltpu.VMEM((256, LOW), bf16), pltpu.VMEM((16, 16, lanes), f32)],
+        compiler_params=pltpu.CompilerParams(vmem_limit_bytes=VMEM_BYTES),
         name="react",
     )(arrived, cells, diffused, deposit, weight, rates)
 

time: 87 us -> 87.9 us (1.010)
  Pallas kernels: 78.9 us -> 87.1 us
  local copies, waits for them, and re-layouts: 6.75 us -> 0 us
    pallas_call x1, Pallas kernels: 59.2 us -> 69.8 us  [local(): pl.pallas_call(functools.partial(exchange_kernel, n_lon, n_lat), out_shap...]
    unnamed x16 -> x0, local copies, waits for them, and re-layouts: 6.75 us -> none
    pallas_call x1, Pallas kernels: 19.7 us -> 17.3 us  [local(): pl.pallas_call(react_kernel, grid=(devices // 16, capacity // lanes), out...]
where the time goes in v3:
time: 87.9 us; the launch traced here: 87.7 us
  Pallas kernels  87.1 us (99%)
    pallas_call x1, Pallas kernels, local(): pl.pallas_call(functools.partial(exchange_kernel, n_lon, n_lat), out_shap...  69.8 us
    pallas_call x1, Pallas kernels, local(): pl.pallas_call(react_kernel, grid=(devices // 16, capacity // lanes), out...  17.3 us

profile of v3, /device:TPU:0, one launch (start us, length us, event | category | flops | bytes accessed | tf_op | source)
XLA Modules:
  0.0 87.7 jit_solution(12781773321319014379)
XLA Ops:
  0.6 69.8 %exchange.1 = (f32[32,16,1024]{2,1,0:T(8,128)}, s32[32,1,1024]{2,1,0:T(1,128)}, f32[4,8,16,128]{3,2,1,0:T(8,128)}, f32[272,256]{1,0:T(8,128)}, bf16[256,256]{1,0:T(8,128)(2,1)}, /*index=5*/f32[2,128,128]{2,1,0:T(8,128)}) custom-call(f32[32,16,1024]{2,1,0:T(8,128)} %species_hbm.1, s32[32,1024]{1,0:T(8,128)} %cells_hbm.1, s32[32]{0:T(128)} %counts_hbm.1, ...), custom_call_target="tpu_custom_call" | custom-call | tf_op jit(solution)/shard_map/exchange/pallas_call | solution.py:431
  70.4 17.3 %react.1 = (f32[32,16,1024]{2,1,0:T(8,128)}, f32[16,8,4,128]{3,2,1,0:T(4,128)}) custom-call(f32[32,16,1024]{2,1,0:T(8,128)} %get-tuple-element.8.arrived_ref, s32[32,1,1024]{2,1,0:T(1,128)} %get-tuple-element.9.cells_ref, f32[4,8,16,128]{3,2,1,0:T(8,128)} %get-tuple-element.10.diffused_ref, f32[272,256]{1,0:T(8,128)} %get-tuple-element.11.deposit_ref, ...), custom_call_target="tpu_custom_call" | custom-call | tf_op jit(solution)/shard_map/react/pallas_call | solution.py:487

commit v4 on v3

--- a/solution.py
+++ b/solution.py
@@ -9,7 +9,8 @@
 
 ITERS = 4
 LOW = 256
-WINDOW = 31
+WINDOW = 8
+LANES = 512
 VMEM_BYTES = 62 * 1024 * 1024
 
 grid_weight = 0.5
@@ -30,7 +31,7 @@
     )
 
 
-def exchange_kernel(
+def step_kernel(
     n_lon,
     n_lat,
     species_hbm,
@@ -41,12 +42,14 @@
     prod_hbm,
     loss_hbm,
     self_hbm,
-    arrived_out,
-    cells_out,
+    parcels_hbm,
+    mixed_ref,
     diffused_out,
     deposit_out,
     weight_out,
     rates_out,
+    hot_out,
+    coarse,
     cells_ref,
     counts_ref,
     grid_ref,
@@ -69,7 +72,6 @@
     send_cell_sem,
     recv_cell_sem,
     out_sem,
-    out_cell_sem,
     halo_send,
     halo_recv,
 ):
@@ -82,8 +84,10 @@
 
     def partner(step, sign):
         a = step // n_lat
-        b = lax.rem(step, n_lat)
+        past = (a + n_lon - 1) // n_lon
         to_lon = lax.rem(lon + sign * a + n_lon, n_lon)
+        source_lon = lon if sign > 0 else to_lon
+        b = lax.rem(step + (n_lat // 2) * past * lax.rem(source_lon, 2), n_lat)
         to_lat = lax.rem(lat + sign * b + n_lat, n_lat)
         return to_lon, to_lat, to_lon * n_lat + to_lat
 
@@ -253,15 +257,12 @@
             + [jnp.where(high == rows, jnp.ones_like(zero), zero)],
             axis=0,
         )
+        hot_out[tile] = low_hot
         deposit_out[...] += lax.dot_general(
             spread, low_hot, (((1,), (1,)), ((), ())), preferred_element_type=f32
         )
 
-    def keep(tile):
-        pltpu.make_async_copy(arrived.at[tile], arrived_out.at[tile], out_sem.at[tile]).start()
-        pltpu.make_async_copy(cells_in.at[tile], cells_out.at[tile], out_cell_sem.at[tile]).start()
-
-    def receive(step, carry):
+    def receive(step):
         from_lon, from_lat, tile = partner(step, -1)
         pltpu.make_async_remote_copy(
             src_ref=marked.at[tile],
@@ -279,12 +280,10 @@
             device_id=(from_lon, from_lat),
             device_id_type=MESH,
         ).wait_recv()
-        keep(tile)
         deposit(tile)
-        return carry
 
     def receive_send(step, carry):
-        receive(step, carry)
+        receive(step)
 
         @pl.when(step + WINDOW < devices)
         def refill():
@@ -318,7 +317,6 @@
     deposit_out[...] = jnp.zeros_like(deposit_out)
     cells_in[me] = marked[me]
     own.wait()
-    keep(me)
     deposit(me)
 
     first = devices // 4
@@ -330,6 +328,88 @@
     diffuse(1, store_out)
     lax.fori_loop(second, devices, receive_send, 0)
 
+    for h in range(16):
+        for side in range(2):
+            lanes = slice(128 * side, 128 * (side + 1))
+            j = 2 * (h % 2) + side
+            number = deposit_out[256 + h : 257 + h, lanes]
+            value = (
+                diffused_out[j, h // 2] + grid_weight * deposit_out[16 * h : 16 * (h + 1), lanes]
+            ) / (1.0 + grid_weight * number)
+            mixed_ref[:, h // 2, j, :] = value
+            coarse[16 * h : 16 * (h + 1), lanes] = value.astype(bf16)
+
+    chunk = min(capacity, 256)
+    chunks = [slice(k, k + chunk) for k in range(0, capacity, chunk)]
+
+    def blend(tile, carry):
+        for where in chunks:
+            cells = cells_in[tile, :, where]
+            picked = jnp.dot(coarse[...], hot_out[tile, :, where], preferred_element_type=f32)
+            high = jnp.broadcast_to(lax.shift_right_arithmetic(cells, 8), (16, chunk))
+            found = picked[:16]
+            for h in range(1, 16):
+                found = jnp.where(high == h, picked[16 * h : 16 * (h + 1)], found)
+            start = arrived[tile, :, where]
+            arrived[tile, :, where] = start + parcel_pull * (found - start)
+        return carry
+
+    lanes = min(capacity, LANES)
+    parts_of = capacity // lanes
+    loss = jnp.concatenate([rates_out[0]] * (chunk // 128), axis=1)
+    self_loss = jnp.concatenate([rates_out[1]] * (chunk // 128), axis=1)
+
+    def out_copy(turn):
+        tiles = pl.ds(16 * (turn // parts_of), 16)
+        where = pl.ds(pl.multiple_of(lax.rem(turn, parts_of) * lanes, 128), lanes)
+        return pltpu.make_async_copy(
+            arrived.at[tiles, :, where], parcels_hbm.at[tiles, :, where], out_sem.at[turn]
+        )
+
+    def react(turn, carry):
+        tile = 16 * (turn // parts_of)
+        base = lax.rem(turn, parts_of) * lanes
+        groups = [
+            (tile + first, pl.ds(pl.multiple_of(base + k, 128), chunk))
+            for k in range(0, lanes, chunk)
+            for first in (0, 8)
+        ]
+        starts = [
+            arrived[pl.ds(first, 8), :, where].reshape(128, chunk) for first, where in groups
+        ]
+        states = starts
+        for sweep in range(ITERS):
+            parts = []
+            for state in states:
+                high_part = state.astype(bf16)
+                low_part = (state - high_part.astype(f32)).astype(bf16)
+                parts.append(jnp.concatenate([high_part, low_part], axis=0))
+            products = [
+                jnp.dot(weight_out[...], part, preferred_element_type=f32) for part in parts
+            ]
+            later = []
+            for start, state, product in zip(starts, states, products):
+                produced = start + (product[:128] + product[128:])
+                bottom = loss + self_loss * state
+                inverse = pl.reciprocal(bottom, approx=True)
+                later.append(produced * (inverse * (2.0 - bottom * inverse)))
+            states = later
+        for (first, where), state in zip(groups, states):
+            for k in range(8):
+                alive = jnp.broadcast_to(cells_in[first + k, :, where] >= 0, (16, chunk))
+                arrived[first + k, :, where] = jnp.where(
+                    alive, state[16 * k : 16 * (k + 1)], 0.0
+                )
+        out_copy(turn).start()
+        return carry
+
+    def group_of_tiles(group, carry):
+        lax.fori_loop(16 * group, 16 * (group + 1), blend, 0)
+        lax.fori_loop(group * parts_of, (group + 1) * parts_of, react, 0)
+        return carry
+
+    lax.fori_loop(0, devices // 16, group_of_tiles, 0)
+
     def finish(step, carry):
         to_lon, to_lat, tile = partner(step, 1)
         cells_copy(to_lon, to_lat, tile).wait_send()
@@ -338,86 +418,11 @@
 
     lax.fori_loop(1, devices, finish, 0)
 
-    def finish_keep(tile, carry):
-        pltpu.make_async_copy(arrived.at[tile], arrived_out.at[tile], out_sem.at[tile]).wait()
-        pltpu.make_async_copy(cells_in.at[tile], cells_out.at[tile], out_cell_sem.at[tile]).wait()
-        return carry
-
-    lax.fori_loop(0, devices, finish_keep, 0)
-
-
-def react_kernel(
-    arrived_ref,
-    cells_ref,
-    diffused_ref,
-    deposit_ref,
-    weight_ref,
-    rates_ref,
-    parcels_ref,
-    mixed_ref,
-    coarse,
-    blended,
-):
-    @pl.when((pl.program_id(0) == 0) & (pl.program_id(1) == 0))
-    def mix():
-        for h in range(16):
-            for side in range(2):
-                lanes = slice(128 * side, 128 * (side + 1))
-                j = 2 * (h % 2) + side
-                number = deposit_ref[256 + h : 257 + h, lanes]
-                value = (
-                    diffused_ref[j, h // 2]
-                    + grid_weight * deposit_ref[16 * h : 16 * (h + 1), lanes]
-                ) / (1.0 + grid_weight * number)
-                mixed_ref[:, h // 2, j, :] = value
-                coarse[16 * h : 16 * (h + 1), lanes] = value.astype(bf16)
-
-    lanes = arrived_ref.shape[2]
-    chunk = min(lanes, 256)
-    chunks = [slice(k, k + chunk) for k in range(0, lanes, chunk)]
-    loss = jnp.concatenate([rates_ref[0]] * (chunk // 128), axis=1)
-    self_loss = jnp.concatenate([rates_ref[1]] * (chunk // 128), axis=1)
-
-    def blend(source, carry):
-        for where in chunks:
-            cells = cells_ref[source, :, where]
-            low_hot = hot_rows(lax.bitwise_and(cells, LOW - 1), LOW)
-            picked = jnp.dot(coarse[...], low_hot, preferred_element_type=f32)
-            high = jnp.broadcast_to(lax.shift_right_arithmetic(cells, 8), (16, chunk))
-            found = picked[:16]
-            for h in range(1, 16):
-                found = jnp.where(high == h, picked[16 * h : 16 * (h + 1)], found)
-            start = arrived_ref[source, :, where]
-            blended[source, :, where] = start + parcel_pull * (found - start)
-        return carry
-
-    lax.fori_loop(0, 16, blend, 0, unroll=2)
-
-    groups = [(first, where) for where in chunks for first in (0, 8)]
-    starts = [
-        blended[first : first + 8, :, where].reshape(128, chunk) for first, where in groups
-    ]
-    states = starts
-    for sweep in range(ITERS):
-        parts = []
-        for state in states:
-            high_part = state.astype(bf16)
-            low_part = (state - high_part.astype(f32)).astype(bf16)
-            parts.append(jnp.concatenate([high_part, low_part], axis=0))
-        products = [jnp.dot(weight_ref[...], part, preferred_element_type=f32) for part in parts]
-        later = []
-        for start, state, product in zip(starts, states, products):
-            produced = start + (product[:128] + product[128:])
-            bottom = loss + self_loss * state
-            inverse = pl.reciprocal(bottom, approx=True)
-            later.append(produced * (inverse * (2.0 - bottom * inverse)))
-        states = later
-    for (first, where), state in zip(groups, states):
-        for k in range(8):
-            alive = jnp.broadcast_to(cells_ref[first + k, :, where] >= 0, (16, chunk))
-            parcels_ref[first + k, :, where] = jnp.where(
-                alive, state[16 * k : 16 * (k + 1)], 0.0
-            )
+    def finish_out(turn, carry):
+        out_copy(turn).wait()
+        return carry
+
+    lax.fori_loop(0, devices // 16 * parts_of, finish_out, 0)
 
 
 def local(
@@ -426,21 +431,22 @@
     n_lon = lax.axis_size("lon")
     n_lat = lax.axis_size("lat")
     devices, species_count, capacity = send_species.shape
-    vmem = pl.BlockSpec(memory_space=pltpu.VMEM)
     hbm = pl.BlockSpec(memory_space=pl.ANY)
-    arrived, cells, diffused, deposit, weight, rates = pl.pallas_call(
-        functools.partial(exchange_kernel, n_lon, n_lat),
+    return pl.pallas_call(
+        functools.partial(step_kernel, n_lon, n_lat),
         out_shape=(
-            jax.ShapeDtypeStruct((devices, species_count, capacity), f32),
-            jax.ShapeDtypeStruct((devices, 1, capacity), jnp.int32),
-            jax.ShapeDtypeStruct((4, 8, 16, 128), f32),
-            jax.ShapeDtypeStruct((272, LOW), f32),
-            jax.ShapeDtypeStruct((256, 256), bf16),
-            jax.ShapeDtypeStruct((2, 128, 128), f32),
+            jax.ShapeDtypeStruct(send_species.shape, f32),
+            jax.ShapeDtypeStruct(grid_state.shape, f32),
         ),
-        in_specs=[pl.BlockSpec(memory_space=pltpu.HBM)] * 8,
-        out_specs=(hbm, hbm, vmem, vmem, vmem, vmem),
+        in_specs=[hbm] * 8,
+        out_specs=(hbm, pl.BlockSpec(memory_space=pltpu.VMEM)),
         scratch_shapes=[
+            pltpu.VMEM((4, 8, 16, 128), f32),
+            pltpu.VMEM((272, LOW), f32),
+            pltpu.VMEM((256, 256), bf16),
+            pltpu.VMEM((2, 128, 128), f32),
+            pltpu.VMEM((devices, LOW, capacity), bf16),
+            pltpu.VMEM((256, LOW), bf16),
             pltpu.VMEM(send_cells.shape, jnp.int32),
             pltpu.SMEM(send_counts.shape, jnp.int32),
             pltpu.VMEM(grid_state.shape, f32),
@@ -462,15 +468,14 @@
             pltpu.SemaphoreType.DMA((devices,)),
             pltpu.SemaphoreType.DMA((devices,)),
             pltpu.SemaphoreType.DMA((devices,)),
-            pltpu.SemaphoreType.DMA((devices,)),
-            pltpu.SemaphoreType.DMA((devices,)),
+            pltpu.SemaphoreType.DMA((devices // 16 * (capacity // min(capacity, LANES)),)),
             pltpu.SemaphoreType.DMA((2, 4)),
             pltpu.SemaphoreType.DMA((2, 4)),
         ],
         compiler_params=pltpu.CompilerParams(
             collective_id=0, has_side_effects=True, vmem_limit_bytes=VMEM_BYTES
         ),
-        name="exchange",
+        name="step",
     )(
         send_species,
         send_cells,
@@ -481,32 +486,6 @@
         loss_rate.reshape(1, 16),
         self_rate.reshape(1, 16),
     )
-
-    lanes = min(capacity, 512)
-    whole = lambda shape: pl.BlockSpec(shape, lambda g, k: (0,) * len(shape))
-    return pl.pallas_call(
-        react_kernel,
-        grid=(devices // 16, capacity // lanes),
-        out_shape=(
-            jax.ShapeDtypeStruct(send_species.shape, f32),
-            jax.ShapeDtypeStruct(grid_state.shape, f32),
-        ),
-        in_specs=[
-            pl.BlockSpec((16, 16, lanes), lambda g, k: (g, 0, k)),
-            pl.BlockSpec((16, 1, lanes), lambda g, k: (g, 0, k)),
-            whole((4, 8, 16, 128)),
-            whole((272, LOW)),
-            whole((256, 256)),
-            whole((2, 128, 128)),
-        ],
-        out_specs=(
-            pl.BlockSpec((16, 16, lanes), lambda g, k: (g, 0, k)),
-            whole(grid_state.shape),
-        ),
-        scratch_shapes=[pltpu.VMEM((256, LOW), bf16), pltpu.VMEM((16, 16, lanes), f32)],
-        compiler_params=pltpu.CompilerParams(vmem_limit_bytes=VMEM_BYTES),
-        name="react",
-    )(arrived, cells, diffused, deposit, weight, rates)
 
 
 def solution(mesh):

time: 87.9 us -> 80.4 us (0.915)
  Pallas kernels: 87.1 us -> 75.7 us
  local copies, waits for them, and re-layouts: 0 us -> 3.91 us
    pallas_call x2 -> x1, Pallas kernels: 87.1 us -> 75.7 us  [local(): pl.pallas_call(functools.partial(step_kernel, n_lon, n_lat), out_shape=(j...]
    unnamed x0 -> x4, local copies, waits for them, and re-layouts: none -> 3.91 us
where the time goes in v4:
time: 80.4 us; the launch traced here: 80.2 us
  Pallas kernels  75.7 us (94%)
  local copies, waits for them, and re-layouts  3.91 us (5%)
    pallas_call x1, Pallas kernels, local(): pl.pallas_call(functools.partial(step_kernel, n_lon, n_lat), out_shape=(j...  75.7 us
    unnamed x4, local copies, waits for them, and re-layouts  3.91 us

profile of v4, /device:TPU:0, one launch (start us, length us, event | category | flops | bytes accessed | tf_op | source)
XLA Modules:
  0.0 80.2 jit_solution(10871379412450289359)
XLA Ops:
  0.6 75.7 %step.1 = (f32[32,16,1024]{2,1,0:T(8,128)}, f32[16,8,4,128]{3,2,1,0:T(4,128)}) custom-call(f32[32,16,1024]{2,1,0:T(8,128)} %species_hbm.1, s32[32,1024]{1,0:T(8,128)} %cells_hbm.1, s32[32]{0:T(128)} %counts_hbm.1, f32[16,8,4,128]{3,2,1,0:T(4,128)} %grid_hbm.1, f32[1,16]{1,0:T(1,128)} %bitcast.3, f32[16,16]{1,0:T(8,128)} %prod_hbm.1, f32[1,16]{1,0:T(1,128)} %bitcast.4, ...), custom_call_target="tpu_custom_call" | custom-call | tf_op jit(solution)/shard_map/step/pallas_call | solution.py:435
  76.3 0.0 copy-start
  76.3 3.2 %copy.12 = f32[32,16,1024]{2,1,0:T(8,128)} copy(f32[32,16,1024]{2,1,0:T(8,128)} %get-tuple-element.4) | data formatting | bytes 4194304
  79.5 0.0 copy-done
  79.5 0.7 copy.13
Async XLA Ops:
  76.3 3.2 %copy-start = (f32[16,8,4,128]{3,2,1,0:T(4,128)S(1)}, f32[16,8,4,128]{3,2,1,0:T(4,128)}, u32[]{:S(2)}) copy-start(f32[16,8,4,128]{3,2,1,0:T(4,128)} %get-tuple-element.5) | copy-start | bytes 786436

commit v5 on v3

--- a/solution.py
+++ b/solution.py
@@ -9,7 +9,7 @@
 
 ITERS = 4
 LOW = 256
-WINDOW = 31
+WINDOW = 8
 VMEM_BYTES = 62 * 1024 * 1024
 
 grid_weight = 0.5
@@ -82,8 +82,10 @@
 
     def partner(step, sign):
         a = step // n_lat
-        b = lax.rem(step, n_lat)
+        past = (a + n_lon - 1) // n_lon
         to_lon = lax.rem(lon + sign * a + n_lon, n_lon)
+        source_lon = lon if sign > 0 else to_lon
+        b = lax.rem(step + (n_lat // 2) * past * lax.rem(source_lon, 2), n_lat)
         to_lat = lax.rem(lat + sign * b + n_lat, n_lat)
         return to_lon, to_lat, to_lon * n_lat + to_lat
 
@@ -383,15 +385,18 @@
             cells = cells_ref[source, :, where]
             low_hot = hot_rows(lax.bitwise_and(cells, LOW - 1), LOW)
             picked = jnp.dot(coarse[...], low_hot, preferred_element_type=f32)
-            high = jnp.broadcast_to(lax.shift_right_arithmetic(cells, 8), (16, chunk))
-            found = picked[:16]
+            high = jnp.broadcast_to(lax.shift_right_arithmetic(cells, 8), (8, chunk))
+            upper, lower = picked[:8], picked[8:16]
             for h in range(1, 16):
-                found = jnp.where(high == h, picked[16 * h : 16 * (h + 1)], found)
+                here = high == h
+                upper = jnp.where(here, picked[16 * h : 16 * h + 8], upper)
+                lower = jnp.where(here, picked[16 * h + 8 : 16 * h + 16], lower)
+            found = jnp.concatenate([upper, lower], axis=0)
             start = arrived_ref[source, :, where]
             blended[source, :, where] = start + parcel_pull * (found - start)
         return carry
 
-    lax.fori_loop(0, 16, blend, 0, unroll=2)
+    lax.fori_loop(0, 16, blend, 0, unroll=8)
 
     groups = [(first, where) for where in chunks for first in (0, 8)]
     starts = [

time: 87.9 us -> 75.3 us (0.86)
  Pallas kernels: 87.1 us -> 74.5 us
    pallas_call x1, Pallas kernels: 69.8 us -> 61.5 us  [local(): pl.pallas_call(functools.partial(exchange_kernel, n_lon, n_lat), out_shap...]
    pallas_call x1, Pallas kernels: 17.3 us -> 13.1 us  [local(): pl.pallas_call(react_kernel, grid=(devices // 16, capacity // lanes), out...]
where the time goes in v5:
time: 75.3 us; the launch traced here: 75.2 us
  Pallas kernels  74.5 us (99%)
    pallas_call x1, Pallas kernels, local(): pl.pallas_call(functools.partial(exchange_kernel, n_lon, n_lat), out_shap...  61.5 us
    pallas_call x1, Pallas kernels, local(): pl.pallas_call(react_kernel, grid=(devices // 16, capacity // lanes), out...  13.1 us

profile of v5, /device:TPU:0, one launch (start us, length us, event | category | flops | bytes accessed | tf_op | source)
XLA Modules:
  0.0 75.2 jit_solution(13484747347297699136)
XLA Ops:
  0.6 61.5 %exchange.1 = (f32[32,16,1024]{2,1,0:T(8,128)}, s32[32,1,1024]{2,1,0:T(1,128)}, f32[4,8,16,128]{3,2,1,0:T(8,128)}, f32[272,256]{1,0:T(8,128)}, bf16[256,256]{1,0:T(8,128)(2,1)}, /*index=5*/f32[2,128,128]{2,1,0:T(8,128)}) custom-call(f32[32,16,1024]{2,1,0:T(8,128)} %species_hbm.1, s32[32,1024]{1,0:T(8,128)} %cells_hbm.1, s32[32]{0:T(128)} %counts_hbm.1, ...), custom_call_target="tpu_custom_call" | custom-call | tf_op jit(solution)/shard_map/exchange/pallas_call | solution.py:436
  62.1 13.1 %react.1 = (f32[32,16,1024]{2,1,0:T(8,128)}, f32[16,8,4,128]{3,2,1,0:T(4,128)}) custom-call(f32[32,16,1024]{2,1,0:T(8,128)} %get-tuple-element.8.arrived_ref, s32[32,1,1024]{2,1,0:T(1,128)} %get-tuple-element.9.cells_ref, f32[4,8,16,128]{3,2,1,0:T(8,128)} %get-tuple-element.10.diffused_ref, f32[272,256]{1,0:T(8,128)} %get-tuple-element.11.deposit_ref, ...), custom_call_target="tpu_custom_call" | custom-call | tf_op jit(solution)/shard_map/react/pallas_call | solution.py:492

commit v6 on v5

--- a/solution.py
+++ b/solution.py
@@ -10,6 +10,8 @@
 ITERS = 4
 LOW = 256
 WINDOW = 8
+LAG = 2
+CHUNK = 256
 VMEM_BYTES = 62 * 1024 * 1024
 
 grid_weight = 0.5
@@ -263,6 +265,10 @@
         pltpu.make_async_copy(arrived.at[tile], arrived_out.at[tile], out_sem.at[tile]).start()
         pltpu.make_async_copy(cells_in.at[tile], cells_out.at[tile], out_cell_sem.at[tile]).start()
 
+    def kept(tile):
+        pltpu.make_async_copy(arrived.at[tile], arrived_out.at[tile], out_sem.at[tile]).wait()
+        pltpu.make_async_copy(cells_in.at[tile], cells_out.at[tile], out_cell_sem.at[tile]).wait()
+
     def receive(step, carry):
         from_lon, from_lat, tile = partner(step, -1)
         pltpu.make_async_remote_copy(
@@ -285,12 +291,27 @@
         deposit(tile)
         return carry
 
+    def settle(step):
+        to_lon, to_lat, tile = partner(step, 1)
+        cells_copy(to_lon, to_lat, tile).wait_send()
+        species_copy(to_lon, to_lat, tile).wait_send()
+        _, _, tile = partner(step, -1)
+        kept(tile)
+
+    def settle_step(step, carry):
+        settle(step)
+        return carry
+
     def receive_send(step, carry):
         receive(step, carry)
 
         @pl.when(step + WINDOW < devices)
         def refill():
             send(step + WINDOW)
+
+        @pl.when(step > LAG)
+        def earlier():
+            settle(step - LAG)
 
         return carry
 
@@ -332,97 +353,169 @@
     diffuse(1, store_out)
     lax.fori_loop(second, devices, receive_send, 0)
 
-    def finish(step, carry):
-        to_lon, to_lat, tile = partner(step, 1)
-        cells_copy(to_lon, to_lat, tile).wait_send()
-        species_copy(to_lon, to_lat, tile).wait_send()
-        return carry
-
-    lax.fori_loop(1, devices, finish, 0)
-
-    def finish_keep(tile, carry):
-        pltpu.make_async_copy(arrived.at[tile], arrived_out.at[tile], out_sem.at[tile]).wait()
-        pltpu.make_async_copy(cells_in.at[tile], cells_out.at[tile], out_cell_sem.at[tile]).wait()
-        return carry
-
-    lax.fori_loop(0, devices, finish_keep, 0)
+    lax.fori_loop(devices - LAG, devices, settle_step, 0)
+    kept(me)
 
 
 def react_kernel(
+    arrived_hbm,
+    cells_hbm,
+    diffused_hbm,
+    deposit_hbm,
+    weight_hbm,
+    rates_hbm,
+    parcels_hbm,
+    mixed_hbm,
     arrived_ref,
     cells_ref,
     diffused_ref,
     deposit_ref,
     weight_ref,
     rates_ref,
-    parcels_ref,
     mixed_ref,
     coarse,
     blended,
+    load_sem,
+    block_sem,
+    out_sem,
+    mixed_sem,
 ):
-    @pl.when((pl.program_id(0) == 0) & (pl.program_id(1) == 0))
-    def mix():
-        for h in range(16):
-            for side in range(2):
-                lanes = slice(128 * side, 128 * (side + 1))
-                j = 2 * (h % 2) + side
-                number = deposit_ref[256 + h : 257 + h, lanes]
-                value = (
-                    diffused_ref[j, h // 2]
-                    + grid_weight * deposit_ref[16 * h : 16 * (h + 1), lanes]
-                ) / (1.0 + grid_weight * number)
-                mixed_ref[:, h // 2, j, :] = value
-                coarse[16 * h : 16 * (h + 1), lanes] = value.astype(bf16)
-
-    lanes = arrived_ref.shape[2]
-    chunk = min(lanes, 256)
-    chunks = [slice(k, k + chunk) for k in range(0, lanes, chunk)]
+    devices, _, capacity = arrived_ref.shape
+    chunk = min(capacity, CHUNK)
+    parts = capacity // chunk
+    groups = devices // 16 * parts
+
+    loads = [
+        pltpu.make_async_copy(source, target, load_sem.at[k])
+        for k, (source, target) in enumerate(
+            (
+                (deposit_hbm, deposit_ref),
+                (diffused_hbm, diffused_ref),
+                (cells_hbm, cells_ref),
+                (weight_hbm, weight_ref),
+                (rates_hbm, rates_ref),
+            )
+        )
+    ]
+    for load in loads:
+        load.start()
+
+    def place(group):
+        first = 16 * (group // parts)
+        lanes = pl.ds(pl.multiple_of(lax.rem(group, parts) * chunk, 128), chunk)
+        return first, lanes
+
+    def block_copy(group):
+        first, lanes = place(group)
+        block = (pl.ds(first, 16), slice(None), lanes)
+        return pltpu.make_async_copy(
+            arrived_hbm.at[block], arrived_ref.at[block], block_sem.at[group]
+        )
+
+    def out_copy(group):
+        first, lanes = place(group)
+        block = (pl.ds(first, 16), slice(None), lanes)
+        return pltpu.make_async_copy(
+            arrived_ref.at[block], parcels_hbm.at[block], out_sem.at[group]
+        )
+
+    def block_start(group, carry):
+        block_copy(group).start()
+        return carry
+
+    lax.fori_loop(0, groups, block_start, 0)
+    loads[0].wait()
+    loads[1].wait()
+
+    for h in range(16):
+        for side in range(2):
+            lanes = slice(128 * side, 128 * (side + 1))
+            j = 2 * (h % 2) + side
+            number = deposit_ref[256 + h : 257 + h, lanes]
+            value = (
+                diffused_ref[j, h // 2] + grid_weight * deposit_ref[16 * h : 16 * (h + 1), lanes]
+            ) / (1.0 + grid_weight * number)
+            mixed_ref[:, h // 2, j, :] = value
+            coarse[16 * h : 16 * (h + 1), lanes] = value.astype(bf16)
+    mixed_copy = pltpu.make_async_copy(mixed_ref, mixed_hbm, mixed_sem)
+    mixed_copy.start()
+    for load in loads[2:]:
+        load.wait()
+
     loss = jnp.concatenate([rates_ref[0]] * (chunk // 128), axis=1)
     self_loss = jnp.concatenate([rates_ref[1]] * (chunk // 128), axis=1)
 
-    def blend(source, carry):
-        for where in chunks:
-            cells = cells_ref[source, :, where]
-            low_hot = hot_rows(lax.bitwise_and(cells, LOW - 1), LOW)
-            picked = jnp.dot(coarse[...], low_hot, preferred_element_type=f32)
-            high = jnp.broadcast_to(lax.shift_right_arithmetic(cells, 8), (8, chunk))
-            upper, lower = picked[:8], picked[8:16]
-            for h in range(1, 16):
-                here = high == h
-                upper = jnp.where(here, picked[16 * h : 16 * h + 8], upper)
-                lower = jnp.where(here, picked[16 * h + 8 : 16 * h + 16], lower)
-            found = jnp.concatenate([upper, lower], axis=0)
-            start = arrived_ref[source, :, where]
-            blended[source, :, where] = start + parcel_pull * (found - start)
-        return carry
-
-    lax.fori_loop(0, 16, blend, 0, unroll=8)
-
-    groups = [(first, where) for where in chunks for first in (0, 8)]
-    starts = [
-        blended[first : first + 8, :, where].reshape(128, chunk) for first, where in groups
-    ]
-    states = starts
-    for sweep in range(ITERS):
-        parts = []
-        for state in states:
+    def blend(group, source):
+        first, lanes = place(group)
+        cells = cells_ref[first + source, :, lanes]
+        low_hot = hot_rows(lax.bitwise_and(cells, LOW - 1), LOW)
+        picked = jnp.dot(coarse[...], low_hot, preferred_element_type=f32)
+        high = jnp.broadcast_to(lax.shift_right_arithmetic(cells, 8), (8, chunk))
+        upper, lower = picked[:8], picked[8:16]
+        for h in range(1, 16):
+            here = high == h
+            upper = jnp.where(here, picked[16 * h : 16 * h + 8], upper)
+            lower = jnp.where(here, picked[16 * h + 8 : 16 * h + 16], lower)
+        found = jnp.concatenate([upper, lower], axis=0)
+        start = arrived_ref[first + source, :, lanes]
+        blended[group, 16 * source : 16 * (source + 1), :] = start + parcel_pull * (found - start)
+
+    def sweep(group, states):
+        later = []
+        for k, state in enumerate(states):
             high_part = state.astype(bf16)
             low_part = (state - high_part.astype(f32)).astype(bf16)
-            parts.append(jnp.concatenate([high_part, low_part], axis=0))
-        products = [jnp.dot(weight_ref[...], part, preferred_element_type=f32) for part in parts]
-        later = []
-        for start, state, product in zip(starts, states, products):
-            produced = start + (product[:128] + product[128:])
+            product = jnp.dot(
+                weight_ref[...],
+                jnp.concatenate([high_part, low_part], axis=0),
+                preferred_element_type=f32,
+            )
+            produced = blended[group, 128 * k : 128 * (k + 1), :] + (
+                product[:128] + product[128:]
+            )
             bottom = loss + self_loss * state
             inverse = pl.reciprocal(bottom, approx=True)
             later.append(produced * (inverse * (2.0 - bottom * inverse)))
-        states = later
-    for (first, where), state in zip(groups, states):
-        for k in range(8):
-            alive = jnp.broadcast_to(cells_ref[first + k, :, where] >= 0, (16, chunk))
-            parcels_ref[first + k, :, where] = jnp.where(
-                alive, state[16 * k : 16 * (k + 1)], 0.0
+        return later
+
+    def begin(group):
+        return [blended[group, 128 * k : 128 * (k + 1), :] for k in range(2)]
+
+    def finish(group, states):
+        first, lanes = place(group)
+        for k in range(16):
+            alive = jnp.broadcast_to(cells_ref[first + k, :, lanes] >= 0, (16, chunk))
+            arrived_ref[first + k, :, lanes] = jnp.where(
+                alive, states[k // 8][16 * (k % 8) : 16 * (k % 8 + 1)], 0.0
             )
+        out_copy(group).start()
+
+    block_copy(0).wait()
+    for source in range(16):
+        blend(0, source)
+
+    def both(group, carry):
+        block_copy(group).wait()
+        states = begin(group - 1)
+        for source in range(16):
+            blend(group, source)
+            if source % 4 == 3:
+                states = sweep(group - 1, states)
+        finish(group - 1, states)
+        return carry
+
+    lax.fori_loop(1, groups, both, 0)
+    states = begin(groups - 1)
+    for _ in range(ITERS):
+        states = sweep(groups - 1, states)
+    finish(groups - 1, states)
+
+    def out_wait(group, carry):
+        out_copy(group).wait()
+        return carry
+
+    lax.fori_loop(0, groups, out_wait, 0)
+    mixed_copy.wait()
 
 
 def local(
@@ -487,28 +580,31 @@
         self_rate.reshape(1, 16),
     )
 
-    lanes = min(capacity, 512)
-    whole = lambda shape: pl.BlockSpec(shape, lambda g, k: (0,) * len(shape))
+    chunk = min(capacity, CHUNK)
+    groups = devices // 16 * (capacity // chunk)
     return pl.pallas_call(
         react_kernel,
-        grid=(devices // 16, capacity // lanes),
         out_shape=(
             jax.ShapeDtypeStruct(send_species.shape, f32),
             jax.ShapeDtypeStruct(grid_state.shape, f32),
         ),
-        in_specs=[
-            pl.BlockSpec((16, 16, lanes), lambda g, k: (g, 0, k)),
-            pl.BlockSpec((16, 1, lanes), lambda g, k: (g, 0, k)),
-            whole((4, 8, 16, 128)),
-            whole((272, LOW)),
-            whole((256, 256)),
-            whole((2, 128, 128)),
+        in_specs=[hbm] * 6,
+        out_specs=(hbm, hbm),
+        scratch_shapes=[
+            pltpu.VMEM(send_species.shape, f32),
+            pltpu.VMEM((devices, 1, capacity), jnp.int32),
+            pltpu.VMEM((4, 8, 16, 128), f32),
+            pltpu.VMEM((272, LOW), f32),
+            pltpu.VMEM((256, 256), bf16),
+            pltpu.VMEM((2, 128, 128), f32),
+            pltpu.VMEM(grid_state.shape, f32),
+            pltpu.VMEM((256, LOW), bf16),
+            pltpu.VMEM((groups, 256, chunk), f32),
+            pltpu.SemaphoreType.DMA((5,)),
+            pltpu.SemaphoreType.DMA((groups,)),
+            pltpu.SemaphoreType.DMA((groups,)),
+            pltpu.SemaphoreType.DMA,
         ],
-        out_specs=(
-            pl.BlockSpec((16, 16, lanes), lambda g, k: (g, 0, k)),
-            whole(grid_state.shape),
-        ),
-        scratch_shapes=[pltpu.VMEM((256, LOW), bf16), pltpu.VMEM((16, 16, lanes), f32)],
         compiler_params=pltpu.CompilerParams(vmem_limit_bytes=VMEM_BYTES),
         name="react",
     )(arrived, cells, diffused, deposit, weight, rates)

time: 75.3 us -> 73.1 us (0.971)
  Pallas kernels: 74.5 us -> 72.4 us
    pallas_call x1, Pallas kernels: 13.1 us -> 11.6 us  [local(): pl.pallas_call(react_kernel, out_shape=(jax.ShapeDtypeStruct(send_species...]
where the time goes in v6:
time: 73.1 us; the launch traced here: 73 us
  Pallas kernels  72.4 us (99%)
    pallas_call x1, Pallas kernels, local(): pl.pallas_call(functools.partial(exchange_kernel, n_lon, n_lat), out_shap...  60.7 us
    pallas_call x1, Pallas kernels, local(): pl.pallas_call(react_kernel, out_shape=(jax.ShapeDtypeStruct(send_species...  11.6 us

profile of v6, /device:TPU:0, one launch (start us, length us, event | category | flops | bytes accessed | tf_op | source)
XLA Modules:
  0.0 73.0 jit_solution(4061407264229551702)
XLA Ops:
  0.6 60.7 %exchange.1 = (f32[32,16,1024]{2,1,0:T(8,128)}, s32[32,1,1024]{2,1,0:T(1,128)}, f32[4,8,16,128]{3,2,1,0:T(8,128)}, f32[272,256]{1,0:T(8,128)}, bf16[256,256]{1,0:T(8,128)(2,1)}, /*index=5*/f32[2,128,128]{2,1,0:T(8,128)}) custom-call(f32[32,16,1024]{2,1,0:T(8,128)} %species_hbm.1, s32[32,1024]{1,0:T(8,128)} %cells_hbm.1, s32[32]{0:T(128)} %counts_hbm.1, ...), custom_call_target="tpu_custom_call" | custom-call | tf_op jit(solution)/shard_map/exchange/pallas_call | solution.py:529
  61.4 11.6 %react.1 = (f32[32,16,1024]{2,1,0:T(8,128)}, f32[16,8,4,128]{3,2,1,0:T(4,128)}) custom-call(f32[32,16,1024]{2,1,0:T(8,128)} %get-tuple-element.8.arrived_hbm, s32[32,1,1024]{2,1,0:T(1,128)} %get-tuple-element.9.cells_hbm, f32[4,8,16,128]{3,2,1,0:T(8,128)} %get-tuple-element.10.diffused_hbm, f32[272,256]{1,0:T(8,128)} %get-tuple-element.11.deposit_hbm, ...), custom_call_target="tpu_custom_call" | custom-call | tf_op jit(solution)/shard_map/react/pallas_call | solution.py:585

commit v7 on v6

--- a/solution.py
+++ b/solution.py
@@ -9,7 +9,7 @@
 
 ITERS = 4
 LOW = 256
-WINDOW = 8
+WINDOW = 4
 LAG = 2
 CHUNK = 256
 VMEM_BYTES = 62 * 1024 * 1024
@@ -45,10 +45,15 @@
     self_hbm,
     arrived_out,
     cells_out,
+    diffused_hbm,
+    deposit_hbm,
+    weight_hbm,
+    rates_hbm,
     diffused_out,
     deposit_out,
     weight_out,
     rates_out,
+    result_sem,
     cells_ref,
     counts_ref,
     grid_ref,
@@ -107,6 +112,17 @@
     ]
     for load in loads:
         load.start()
+    results = [
+        pltpu.make_async_copy(source, target, result_sem.at[k])
+        for k, (source, target) in enumerate(
+            (
+                (weight_out, weight_hbm),
+                (rates_out, rates_hbm),
+                (diffused_out, diffused_hbm),
+                (deposit_out, deposit_hbm),
+            )
+        )
+    ]
     barrier = pltpu.get_barrier_semaphore()
 
     def greet(step, carry):
@@ -338,6 +354,9 @@
     rates_out[0] = jnp.concatenate([1.0 + column(loss_ref[...], 128)] * 8, axis=0)
     rates_out[1] = jnp.concatenate([column(self_ref[...], 128)] * 8, axis=0)
 
+    results[0].start()
+    results[1].start()
+
     deposit_out[...] = jnp.zeros_like(deposit_out)
     cells_in[me] = marked[me]
     own.wait()
@@ -351,10 +370,14 @@
     halo_start(1)
     lax.fori_loop(first, second, receive_send, 0)
     diffuse(1, store_out)
+    results[2].start()
     lax.fori_loop(second, devices, receive_send, 0)
 
+    results[3].start()
     lax.fori_loop(devices - LAG, devices, settle_step, 0)
     kept(me)
+    for result in results:
+        result.wait()
 
 
 def react_kernel(
@@ -524,7 +547,6 @@
     n_lon = lax.axis_size("lon")
     n_lat = lax.axis_size("lat")
     devices, species_count, capacity = send_species.shape
-    vmem = pl.BlockSpec(memory_space=pltpu.VMEM)
     hbm = pl.BlockSpec(memory_space=pl.ANY)
     arrived, cells, diffused, deposit, weight, rates = pl.pallas_call(
         functools.partial(exchange_kernel, n_lon, n_lat),
@@ -537,8 +559,13 @@
             jax.ShapeDtypeStruct((2, 128, 128), f32),
         ),
         in_specs=[pl.BlockSpec(memory_space=pltpu.HBM)] * 8,
-        out_specs=(hbm, hbm, vmem, vmem, vmem, vmem),
+        out_specs=(hbm,) * 6,
         scratch_shapes=[
+            pltpu.VMEM((4, 8, 16, 128), f32),
+            pltpu.VMEM((272, LOW), f32),
+            pltpu.VMEM((256, 256), bf16),
+            pltpu.VMEM((2, 128, 128), f32),
+            pltpu.SemaphoreType.DMA((4,)),
             pltpu.VMEM(send_cells.shape, jnp.int32),
             pltpu.SMEM(send_counts.shape, jnp.int32),
             pltpu.VMEM(grid_state.shape, f32),

time: 73.1 us -> 76.1 us (1.041)
  Pallas kernels: 72.4 us -> 75.2 us
    pallas_call x1, Pallas kernels: 60.7 us -> 63.6 us  [local(): pl.pallas_call(functools.partial(exchange_kernel, n_lon, n_lat), out_shap...]
where the time goes in v7:
time: 76.1 us; the launch traced here: 75.9 us
  Pallas kernels  75.2 us (99%)
    pallas_call x1, Pallas kernels, local(): pl.pallas_call(functools.partial(exchange_kernel, n_lon, n_lat), out_shap...  63.6 us
    pallas_call x1, Pallas kernels, local(): pl.pallas_call(react_kernel, out_shape=(jax.ShapeDtypeStruct(send_species...  11.6 us

profile of v7, /device:TPU:0, one launch (start us, length us, event | category | flops | bytes accessed | tf_op | source)
XLA Modules:
  0.0 75.9 jit_solution(4956748542714042516)
XLA Ops:
  0.6 63.6 %exchange.1 = (f32[32,16,1024]{2,1,0:T(8,128)}, s32[32,1,1024]{2,1,0:T(1,128)}, f32[4,8,16,128]{3,2,1,0:T(8,128)}, f32[272,256]{1,0:T(8,128)}, bf16[256,256]{1,0:T(8,128)(2,1)}, /*index=5*/f32[2,128,128]{2,1,0:T(8,128)}) custom-call(f32[32,16,1024]{2,1,0:T(8,128)} %species_hbm.1, s32[32,1024]{1,0:T(8,128)} %cells_hbm.1, s32[32]{0:T(128)} %counts_hbm.1, ...), custom_call_target="tpu_custom_call" | custom-call | tf_op jit(solution)/shard_map/exchange/pallas_call | solution.py:551
  64.2 11.6 %react.1 = (f32[32,16,1024]{2,1,0:T(8,128)}, f32[16,8,4,128]{3,2,1,0:T(4,128)}) custom-call(f32[32,16,1024]{2,1,0:T(8,128)} %get-tuple-element.8.arrived_hbm, s32[32,1,1024]{2,1,0:T(1,128)} %get-tuple-element.9.cells_hbm, f32[4,8,16,128]{3,2,1,0:T(8,128)} %get-tuple-element.10.diffused_hbm, f32[272,256]{1,0:T(8,128)} %get-tuple-element.11.deposit_hbm, ...), custom_call_target="tpu_custom_call" | custom-call | tf_op jit(solution)/shard_map/react/pallas_call | solution.py:612

commit v8 on v7

--- a/solution.py
+++ b/solution.py
@@ -9,7 +9,7 @@
 
 ITERS = 4
 LOW = 256
-WINDOW = 4
+WINDOW = 12
 LAG = 2
 CHUNK = 256
 VMEM_BYTES = 62 * 1024 * 1024
@@ -96,6 +96,15 @@
         to_lat = lax.rem(lat + sign * b + n_lat, n_lat)
         return to_lon, to_lat, to_lon * n_lat + to_lat
 
+    barrier = pltpu.get_barrier_semaphore()
+
+    def greet(step, carry):
+        to_lon, to_lat, _ = partner(step, 1)
+        pl.semaphore_signal(barrier, inc=1, device_id=(to_lon, to_lat), device_id_type=MESH)
+        return carry
+
+    lax.fori_loop(1, devices, greet, 0)
+
     loads = [
         pltpu.make_async_copy(source, target, load_sem.at[k])
         for k, (source, target) in enumerate(
@@ -123,15 +132,6 @@
             )
         )
     ]
-    barrier = pltpu.get_barrier_semaphore()
-
-    def greet(step, carry):
-        to_lon, to_lat, _ = partner(step, 1)
-        pl.semaphore_signal(barrier, inc=1, device_id=(to_lon, to_lat), device_id_type=MESH)
-        return carry
-
-    lax.fori_loop(1, devices, greet, 0)
-
     own = pltpu.make_async_copy(species_hbm.at[me], arrived.at[me], recv_sem.at[me])
     own.start()
 
@@ -260,7 +260,7 @@
     def store_out(j, value):
         diffused_out[j] = value
 
-    def deposit(tile):
+    def tables(tile):
         cells = cells_in[tile]
         rounded = arrived[tile].astype(bf16)
         low_hot = hot_rows(lax.bitwise_and(cells, LOW - 1), LOW)
@@ -273,8 +273,16 @@
             + [jnp.where(high == rows, jnp.ones_like(zero), zero)],
             axis=0,
         )
+        return spread, low_hot
+
+    def deposit(one, other):
+        spread_one, hot_one = tables(one)
+        spread_other, hot_other = tables(other)
         deposit_out[...] += lax.dot_general(
-            spread, low_hot, (((1,), (1,)), ((), ())), preferred_element_type=f32
+            jnp.concatenate([spread_one, spread_other], axis=1),
+            jnp.concatenate([hot_one, hot_other], axis=1),
+            (((1,), (1,)), ((), ())),
+            preferred_element_type=f32,
         )
 
     def keep(tile):
@@ -285,7 +293,7 @@
         pltpu.make_async_copy(arrived.at[tile], arrived_out.at[tile], out_sem.at[tile]).wait()
         pltpu.make_async_copy(cells_in.at[tile], cells_out.at[tile], out_cell_sem.at[tile]).wait()
 
-    def receive(step, carry):
+    def receive(step):
         from_lon, from_lat, tile = partner(step, -1)
         pltpu.make_async_remote_copy(
             src_ref=marked.at[tile],
@@ -304,8 +312,7 @@
             device_id_type=MESH,
         ).wait_recv()
         keep(tile)
-        deposit(tile)
-        return carry
+        return tile
 
     def settle(step):
         to_lon, to_lat, tile = partner(step, 1)
@@ -318,16 +325,21 @@
         settle(step)
         return carry
 
-    def receive_send(step, carry):
-        receive(step, carry)
-
-        @pl.when(step + WINDOW < devices)
-        def refill():
-            send(step + WINDOW)
-
-        @pl.when(step > LAG)
-        def earlier():
-            settle(step - LAG)
+    def receive_send(pair, carry):
+        tiles = []
+        for step in (2 * pair, 2 * pair + 1):
+            tiles.append(receive(step))
+
+            @pl.when(step + WINDOW < devices)
+            def refill():
+                send(step + WINDOW)
+
+        deposit(*tiles)
+        for step in (2 * pair, 2 * pair + 1):
+
+            @pl.when(step > LAG)
+            def earlier():
+                settle(step - LAG)
 
         return carry
 
@@ -361,17 +373,19 @@
     cells_in[me] = marked[me]
     own.wait()
     keep(me)
-    deposit(me)
-
-    first = devices // 4
-    second = devices // 2
+    near = receive(1)
+    send(1 + WINDOW)
+    deposit(me, near)
+
+    first = devices // 8
+    second = devices // 4
     lax.fori_loop(1, first, receive_send, 0)
     diffuse(0, store_field)
     halo_start(1)
     lax.fori_loop(first, second, receive_send, 0)
     diffuse(1, store_out)
     results[2].start()
-    lax.fori_loop(second, devices, receive_send, 0)
+    lax.fori_loop(second, devices // 2, receive_send, 0)
 
     results[3].start()
     lax.fori_loop(devices - LAG, devices, settle_step, 0)

time: 76.1 us -> 72 us (0.946)
  Pallas kernels: 75.2 us -> 71.2 us
    pallas_call x1, Pallas kernels: 63.6 us -> 59.6 us  [local(): pl.pallas_call(functools.partial(exchange_kernel, n_lon, n_lat), out_shap...]
where the time goes in v8:
time: 72 us; the launch traced here: 71.8 us
  Pallas kernels  71.2 us (99%)
    pallas_call x1, Pallas kernels, local(): pl.pallas_call(functools.partial(exchange_kernel, n_lon, n_lat), out_shap...  59.6 us
    pallas_call x1, Pallas kernels, local(): pl.pallas_call(react_kernel, out_shape=(jax.ShapeDtypeStruct(send_species...  11.6 us

profile of v8, /device:TPU:0, one launch (start us, length us, event | category | flops | bytes accessed | tf_op | source)
XLA Modules:
  0.0 71.8 jit_solution(18097779973220411001)
XLA Ops:
  0.6 59.6 %exchange.1 = (f32[32,16,1024]{2,1,0:T(8,128)}, s32[32,1,1024]{2,1,0:T(1,128)}, f32[4,8,16,128]{3,2,1,0:T(8,128)}, f32[272,256]{1,0:T(8,128)}, bf16[256,256]{1,0:T(8,128)(2,1)}, /*index=5*/f32[2,128,128]{2,1,0:T(8,128)}) custom-call(f32[32,16,1024]{2,1,0:T(8,128)} %species_hbm.1, s32[32,1024]{1,0:T(8,128)} %cells_hbm.1, s32[32]{0:T(128)} %counts_hbm.1, ...), custom_call_target="tpu_custom_call" | custom-call | tf_op jit(solution)/shard_map/exchange/pallas_call | solution.py:565
  60.2 11.6 %react.1 = (f32[32,16,1024]{2,1,0:T(8,128)}, f32[16,8,4,128]{3,2,1,0:T(4,128)}) custom-call(f32[32,16,1024]{2,1,0:T(8,128)} %get-tuple-element.8.arrived_hbm, s32[32,1,1024]{2,1,0:T(1,128)} %get-tuple-element.9.cells_hbm, f32[4,8,16,128]{3,2,1,0:T(8,128)} %get-tuple-element.10.diffused_hbm, f32[272,256]{1,0:T(8,128)} %get-tuple-element.11.deposit_hbm, ...), custom_call_target="tpu_custom_call" | custom-call | tf_op jit(solution)/shard_map/react/pallas_call | solution.py:626

commit v9 on v8

--- a/solution.py
+++ b/solution.py
@@ -9,7 +9,7 @@
 
 ITERS = 4
 LOW = 256
-WINDOW = 12
+WINDOW = 16
 LAG = 2
 CHUNK = 256
 VMEM_BYTES = 62 * 1024 * 1024
@@ -541,7 +541,7 @@
         finish(group - 1, states)
         return carry
 
-    lax.fori_loop(1, groups, both, 0)
+    lax.fori_loop(1, groups, both, 0, unroll=True)
     states = begin(groups - 1)
     for _ in range(ITERS):
         states = sweep(groups - 1, states)

time: 72 us -> 71.9 us (level)
  no operation moved by 1% of the time
where the time goes in v9:
time: 71.9 us; the launch traced here: 71.7 us
  Pallas kernels  70.9 us (99%)
  between operations  0.8 us (1%)
    pallas_call x1, Pallas kernels, local(): pl.pallas_call(functools.partial(exchange_kernel, n_lon, n_lat), out_shap...  59.6 us
    pallas_call x1, Pallas kernels, local(): pl.pallas_call(react_kernel, out_shape=(jax.ShapeDtypeStruct(send_species...  11.4 us

profile of v9, /device:TPU:0, one launch (start us, length us, event | category | flops | bytes accessed | tf_op | source)
XLA Modules:
  0.0 71.7 jit_solution(838994796002463831)
XLA Ops:
  0.6 59.6 %exchange.1 = (f32[32,16,1024]{2,1,0:T(8,128)}, s32[32,1,1024]{2,1,0:T(1,128)}, f32[4,8,16,128]{3,2,1,0:T(8,128)}, f32[272,256]{1,0:T(8,128)}, bf16[256,256]{1,0:T(8,128)(2,1)}, /*index=5*/f32[2,128,128]{2,1,0:T(8,128)}) custom-call(f32[32,16,1024]{2,1,0:T(8,128)} %species_hbm.1, s32[32,1024]{1,0:T(8,128)} %cells_hbm.1, s32[32]{0:T(128)} %counts_hbm.1, ...), custom_call_target="tpu_custom_call" | custom-call | tf_op jit(solution)/shard_map/exchange/pallas_call | solution.py:565
  60.2 11.4 %react.1 = (f32[32,16,1024]{2,1,0:T(8,128)}, f32[16,8,4,128]{3,2,1,0:T(4,128)}) custom-call(f32[32,16,1024]{2,1,0:T(8,128)} %get-tuple-element.8.arrived_hbm, s32[32,1,1024]{2,1,0:T(1,128)} %get-tuple-element.9.cells_hbm, f32[4,8,16,128]{3,2,1,0:T(8,128)} %get-tuple-element.10.diffused_hbm, f32[272,256]{1,0:T(8,128)} %get-tuple-element.11.deposit_hbm, ...), custom_call_target="tpu_custom_call" | custom-call | tf_op jit(solution)/shard_map/react/pallas_call | solution.py:626
